TPU v7x, 256 devices: a whole 4x4x8 slice. The times are simulated.
256 devices in a mesh: row: 8 (over y, core), col: 32 (over x, z).
Axes of the slice: x: 4, y: 4, z: 8, core: 2. Of those that a mesh axis runs over, the one named last changes fastest.
Arguments:
- matrix: bfloat16 [8, 8, 256, 4, 32, 256], P(None, 'row', None, None, 'col'), as said below
- pattern: int32 [64, 128], replicated, may hold values from 0 to 1, as said below
- panel: int32 [1], replicated, may hold values from 0 to 47
Outputs:
- factored: float32 [8, 8, 256, 4, 32, 256], P(None, 'row', None, None, 'col')
Inputs may be any that keep to these rules, and one draw needn't show every extreme that they name: `pattern`: in every block column, among the block rows held by one grid row (I congruent r modulo 8) at most 5 blocks are nonzero, exactly 5 in the grid row that holds the column's diagonal position; diagonal blocks of the window are always nonzero. `matrix`: diagonal blocks have diagonal entries between 21 and 51.
All inputs are finite; a program needn't handle non-finite values.
Results may differ from a plain program's by a relative error of at most 0.0008.
Values may be sent and summed in bfloat16 or wider, within the bound.
No kernel may reach another device: no remote copies, remote signals or barrier semaphores. Data moves between devices by JAX's collectives and lax.ppermute only.
A program may use at most 64 MiB of HBM per device.

v0:
```python
import jax
import jax.numpy as jnp
from jax import lax
from jax.sharding import PartitionSpec as P

NEWTON = 3


def from_root(value, axis, root):
    mine = lax.axis_index(axis) == root
    return lax.psum(jnp.where(mine, value, jnp.zeros_like(value)), axis)


def newton(pivot_block):
    order_size = pivot_block.shape[0]
    identity = jnp.eye(order_size, dtype=jnp.float32)
    pivots = jnp.diagonal(pivot_block)
    inverse = identity / pivots[None, :]
    for sweep_index in range(NEWTON):
        image = jnp.dot(pivot_block, inverse, precision=lax.Precision.HIGHEST)
        inverse = jnp.dot(inverse, 2.0 * identity - image, precision=lax.Precision.HIGHEST)
    return inverse


def body(matrix, pattern, panel):
    rows_here = lax.axis_size("row")
    cols_here = lax.axis_size("col")
    grid_row = lax.axis_index("row")
    grid_col = lax.axis_index("col")
    block_rows = matrix.shape[0]
    order_size = matrix.shape[2]
    block_cols = matrix.shape[3]
    panel_at = panel[0]
    local_blocks = matrix.reshape(block_rows, order_size, block_cols, order_size)
    row_ids = jnp.arange(block_rows, dtype=jnp.int32) * rows_here + grid_row
    col_ids = jnp.arange(block_cols, dtype=jnp.int32) * cols_here + grid_col
    grid_mask = pattern.reshape(block_rows, rows_here, block_cols, cols_here)
    local_mask = lax.dynamic_index_in_dim(
        lax.dynamic_index_in_dim(grid_mask, grid_row, 1, keepdims=False),
        grid_col,
        2,
        keepdims=False,
    )
    mask_top = lax.dynamic_index_in_dim(pattern, panel_at, 0, keepdims=False).reshape(
        block_cols, cols_here
    )
    mask_top = lax.dynamic_index_in_dim(mask_top, grid_col, 1, keepdims=False)
    mask_left = lax.dynamic_index_in_dim(pattern, panel_at, 1, keepdims=False).reshape(
        block_rows, rows_here
    )
    mask_left = lax.dynamic_index_in_dim(mask_left, grid_row, 1, keepdims=False)
    upper_here = lax.dynamic_index_in_dim(local_blocks, panel_at // rows_here, 0, keepdims=False)
    upper_row = from_root(upper_here, "row", panel_at % rows_here)
    upper_keep = (mask_top * (col_ids > panel_at).astype(jnp.int32)).astype(jnp.bfloat16)
    upper_matrix = (upper_row * upper_keep[None, :, None]).reshape(
        order_size, block_cols * order_size
    )
    pivot_block = lax.dynamic_index_in_dim(upper_row, panel_at // cols_here, 1, keepdims=False)
    panel_column = lax.dynamic_index_in_dim(local_blocks, panel_at // cols_here, 2, keepdims=False)
    lower_keep = mask_left * (row_ids > panel_at).astype(jnp.int32)
    chosen_count = panel_column.shape[0]
    inverse = newton(pivot_block.astype(jnp.float32))
    scaled = (
        panel_column.astype(jnp.float32) * lower_keep.astype(jnp.float32)[:, None, None]
    ).reshape(chosen_count * order_size, order_size)
    lower_here = jnp.dot(scaled, inverse, precision=lax.Precision.HIGHEST).astype(jnp.bfloat16)
    lower_panel = from_root(lower_here, "col", panel_at % cols_here)
    change_rows = jnp.dot(lower_panel, upper_matrix, preferred_element_type=jnp.float32).reshape(
        chosen_count, order_size, block_cols, order_size
    )
    lower_blocks = lower_panel.reshape(chosen_count, order_size, order_size)
    masked_base = (
        local_blocks.astype(jnp.float32) * local_mask.astype(jnp.float32)[:, None, :, None]
    )
    result = masked_base - change_rows
    replaced = jnp.where(
        (row_ids > panel_at)[:, None, None], lower_blocks.astype(jnp.float32), inverse[None, :, :]
    )
    column_hit = (col_ids == panel_at)[None, None, :, None] & (row_ids >= panel_at)[
        :, None, None, None
    ]
    result = jnp.where(column_hit, replaced[:, :, None, :], result)
    return result.reshape(matrix.shape)


def solution(mesh):
    in_specs = (P(None, "row", None, None, "col", None), P(), P())
    out_specs = P(None, "row", None, None, "col", None)
    return jax.shard_map(body, mesh=mesh, in_specs=in_specs, out_specs=out_specs, check_vma=False)
```

profile of v0, /device:TPU:24, one launch (start us, length us, event | category | flops | bytes accessed | tf_op | source)
XLA Modules:
  0.0 265.8 jit_solution(13848374423803764382)
XLA Ops:
  7.2 1.2 constant_dynamic-slice_fusion.2
  8.5 0.9 fusion.6
  9.4 0.9 dynamic-slice_reduce_fusion
  10.5 4.5 %constant_dynamic-slice_fusion.3 = bf16[8,1,256,1,1,256]{5,3,4,2,1,0:T(2,128)(2,1)S(1)} fusion(bf16[8,1,256,4,1,256]{5,3,4,2,1,0:T(4,128)(2,1)} %param.3, s32[]{:T(128)S(6)} %select_n.91), kind=kLoop, calls=%fused_computation.41 | loop fusion | bytes 2097156 | tf_op jit(solution)/shard_map/jit(dynamic_index_in_dim)/dynamic_slice | solution.py:59
  15.0 0.2 dynamic-slice_reduce_fusion.1
  15.3 0.1 reshape.121
  15.5 0.2 dynamic-slice_reduce_fusion.2
  15.8 0.1 copy.25
  15.9 0.2 copy.23
  16.1 59.9 %all-reduce.3.cloned.1.call-done = bf16[256,4,256]{2,0,1:T(8,128)(2,1)} async-done(((bf16[256,4,256]{2,0,1:T(8,128)(2,1)}), bf16[256,4,256]{2,0,1:T(8,128)(2,1)}) %all-reduce.3.cloned.1.call-update) | async-done | bytes 524304 | tf_op jit(solution)/shard_map/psum | solution.py:11
  76.1 1.0 bitcast_convert_fusion
  77.1 2.3 gather_fusion
  79.4 1.2 convolution_subtract_fusion.2
  80.6 0.4 fusion.8
  81.0 1.2 convolution_subtract_fusion.1
  82.2 0.4 fusion.26
  82.6 0.3 convolution_subtract_fusion
  82.9 0.4 fusion.27
  83.3 2.8 %fusion.3 = bf16[2048,256]{1,0:T(8,128)(2,1)} fusion(f32[256,256]{1,0:T(8,128)S(1)} %fusion.27, bf16[2048,256]{1,0:T(8,128)(2,1)S(1)} %bitcast.60, f32[2048]{0:T(1024)S(1)} %bitcast.62, pred[]{:T(512)S(6)} %eq.30), kind=kOutput, calls=%fused_computation.6 | convolution fusion | flops 1612709888 | bytes 2367489 | tf_op jit(solution)/shard_map/dot_general | solution.py:66
  86.5 0.2 copy.20
  86.7 150.6 %all-reduce.5.cloned.1.call-done = bf16[8,256,256]{2,1,0:T(8,128)(2,1)} async-done(((bf16[8,256,256]{2,1,0:T(8,128)(2,1)}), bf16[8,256,256]{2,1,0:T(8,128)(2,1)}) %all-reduce.5.cloned.1.call-update) | async-done | bytes 1048592 | tf_op jit(solution)/shard_map/psum | solution.py:11
  237.2 1.5 convert_select_fusion
  238.7 4.0 %fusion.2 = f32[8,1,256,4,1,256]{5,2,3,0,4,1:T(8,128)S(1)} fusion(bf16[8,1,256,4,1,256]{5,3,4,2,1,0:T(4,128)(2,1)} %param.3, f32[8,4]{1,0:T(8,128)S(1)} %copy.19, f32[8,256,256]{2,1,0:T(8,128)S(1)} %convert_select_fusion, pred[8,4]{1,0:T(8,128)(4,1)S(1)} %broadcast_and_fusion, bf16[8,256,256]{2,1,0:T(8,128)(2,1)} %all-reduce.5.cloned.1.call-done, ...), kind=kOutput, calls=%fused_computation.4 | convolution fusion | flops 1082130432 | bytes 16253088 | tf_op jit(solution)/shard_map/dot_general | solution.py:68
  242.7 16.3 %copy.21 = f32[8,1,256,4,1,256]{5,4,3,2,1,0:T(1,128)} copy(f32[8,1,256,4,1,256]{5,2,3,0,4,1:T(8,128)S(1)} %fusion.2) | data formatting | bytes 16777216 | tf_op jit(solution)/shard_map/reshape | solution.py:83
  (23 shorter events, 0.7 us)
Async XLA Ops:
  6.5 8.7 %copy-start.1 = (s32[64,128]{1,0:T(8,128)S(1)}, s32[64,128]{1,0:T(8,128)}, u32[]{:S(2)}) copy-start(s32[64,128]{1,0:T(8,128)} %param.4) | copy-start | bytes 98308
  6.5 69.5 %all-reduce.3.cloned.1.call-start = ((), (), s32[]{:S(2)}) async-start(), calls=%async_computation | async-start | bytes 1048576 | tf_op jit(solution)/shard_map/psum | solution.py:11
  9.4 227.9 %all-reduce.5.cloned.1.call-start = ((), (), s32[]{:S(2)}) async-start(), calls=%async_computation.1 | async-start | bytes 2097152 | tf_op jit(solution)/shard_map/psum | solution.py:11
  76.1 6.6 %copy-start = (bf16[256,4,256]{2,0,1:T(8,128)(2,1)S(1)}, bf16[256,4,256]{2,0,1:T(8,128)(2,1)}, u32[]{:S(2)}) copy-start(bf16[256,4,256]{2,0,1:T(8,128)(2,1)} %all-reduce.3.cloned.1.call-done) | copy-start | bytes 1572868
Sparse Core Ops, SparseCore 0:
  9.7 66.3 all-reduce.2
  86.3 150.9 all-reduce.4
where the time goes:
time: 266 us
  waiting for transfers between devices  211 us (79%)
  local copies, waits for them, and re-layouts  26.7 us (10%)
  between operations  14.3 us (5%)
  matrix products  10.6 us (4%)
  other arithmetic  3.56 us (1%)
    psum x2, waiting for transfers between devices, from_root(): return lax.psum(jnp.where(mine, value, jnp.zeros_like(value)), axis)  210 us
    reshape x1, local copies, waits for them, and re-layouts, body(): return result.reshape(matrix.shape)  16.3 us
  transfers between devices with their start and end apart: 2, of which 2 were waited for; matrix products, arithmetic and copies ran while one was open for 3% of the time, Pallas kernels for 0%

commit v1 on v0

v1 whole, which is shorter than its diff:
```python
import functools

import jax
import jax.numpy as jnp
from jax import lax
from jax.experimental import pallas as pl
from jax.experimental.pallas import tpu as pltpu
from jax.sharding import PartitionSpec as P

SLOTS = 5
BLK = 256
HI = lax.Precision.HIGHEST


def first(t):
    return t ^ 1


def second(t, n):
    return (t + 1) % n if t % 2 else (t - 1) % n


def second_of(t, n):
    return jnp.where(t % 2 == 1, t + 1, t + n - 1) % n


def spread_rows(block, scratch):
    for half in range(2):
        scratch[:, half * 4 : half * 4 + 4, :] = block[:, :, half * 128 : half * 128 + 128].astype(
            jnp.float32
        )


def pick_column(scratch, at, half):
    flat = scratch.reshape(BLK * 8, 128)
    return flat[pl.ds(half * 4 + at, BLK, stride=8), :].astype(jnp.bfloat16)


def top_kernel(info, block, upper, pivot, scratch):
    spread_rows(block[0], scratch)
    for half in range(2):
        lanes = slice(half * 128, half * 128 + 128)
        for at in range(4):
            upper[at, :, lanes] = pick_column(scratch, at, half)
        pivot[:, lanes] = pick_column(scratch, info[1], half)


def extract_top(matrix, info):
    return pl.pallas_call(
        top_kernel,
        grid_spec=pltpu.PrefetchScalarGridSpec(
            num_scalar_prefetch=1,
            grid=(1,),
            in_specs=[pl.BlockSpec((1, BLK, 4, BLK), lambda s, info: (info[0], 0, 0, 0))],
            out_specs=[
                pl.BlockSpec((4, BLK, BLK), lambda s, info: (0, 0, 0)),
                pl.BlockSpec((BLK, BLK), lambda s, info: (0, 0)),
            ],
            scratch_shapes=[pltpu.VMEM((BLK, 8, 128), jnp.float32)],
        ),
        out_shape=[
            jax.ShapeDtypeStruct((4, BLK, BLK), jnp.bfloat16),
            jax.ShapeDtypeStruct((BLK, BLK), jnp.bfloat16),
        ],
        name="extract_top",
    )(info, matrix)


def left_kernel(info, block, panel, scratch):
    spread_rows(block[0], scratch)
    for half in range(2):
        panel[0, :, half * 128 : half * 128 + 128] = pick_column(scratch, info[1], half)


def extract_left(matrix, info):
    return pl.pallas_call(
        left_kernel,
        grid_spec=pltpu.PrefetchScalarGridSpec(
            num_scalar_prefetch=1,
            grid=(SLOTS,),
            in_specs=[pl.BlockSpec((1, BLK, 4, BLK), lambda s, info: (info[2 + s], 0, 0, 0))],
            out_specs=pl.BlockSpec((1, BLK, BLK), lambda s, info: (s, 0, 0)),
            scratch_shapes=[pltpu.VMEM((BLK, 8, 128), jnp.float32)],
        ),
        out_shape=jax.ShapeDtypeStruct((SLOTS, BLK, BLK), jnp.bfloat16),
        name="extract_left",
    )(info, matrix)


def newton_kernel(pivot, panel, inverse, lower):
    block = pivot[...].astype(jnp.float32)
    down = lax.broadcasted_iota(jnp.int32, (BLK, BLK), 0)
    along = lax.broadcasted_iota(jnp.int32, (BLK, BLK), 1)
    same = down == along
    identity = jnp.where(same, 1.0, 0.0)
    diagonal = jnp.where(same, block, 0.0)
    error = identity - block * (1.0 / jnp.sum(diagonal, axis=0, keepdims=True))
    dot = functools.partial(jnp.dot, precision=HI, preferred_element_type=jnp.float32)
    error2 = dot(error, error)
    error4 = dot(error2, error2)
    left = identity + error
    left = left + dot(left, error2)
    left = left + dot(left, error4)
    result = left * (1.0 / jnp.sum(diagonal, axis=1, keepdims=True))
    inverse[...] = result
    high = result.astype(jnp.bfloat16)
    rest = result - high.astype(jnp.float32)
    middle = rest.astype(jnp.bfloat16)
    low = (rest - middle.astype(jnp.float32)).astype(jnp.bfloat16)
    for slot in range(SLOTS):
        rows = panel[slot]
        total = jnp.dot(rows, low, preferred_element_type=jnp.float32)
        total += jnp.dot(rows, middle, preferred_element_type=jnp.float32)
        total += jnp.dot(rows, high, preferred_element_type=jnp.float32)
        lower[slot] = total.astype(jnp.bfloat16)


def newton_lower(pivot, panel):
    return pl.pallas_call(
        newton_kernel,
        out_shape=[
            jax.ShapeDtypeStruct((BLK, BLK), jnp.float32),
            jax.ShapeDtypeStruct((SLOTS, BLK, BLK), jnp.bfloat16),
        ],
        name="newton_lower",
    )(pivot, panel)


def finish_kernel(mask, slot_of, keep, hit, block, lower, upper, inverse, out):
    row = pl.program_id(0)
    column = lax.broadcasted_iota(jnp.int32, (BLK, 4, 128), 1)
    on = jnp.zeros((BLK, 4, 128), jnp.int32)
    for at in range(4):
        on = jnp.where(column == at, mask[row * 4 + at], on)
    wide = out.reshape(BLK, 8, 128)
    for half in range(2):
        piece = block[0, :, :, half * 128 : half * 128 + 128].astype(jnp.float32)
        wide[:, pl.ds(half, 4, stride=2), :] = jnp.where(on != 0, piece, 0.0)
    slot = slot_of[row]

    for at in range(4):

        @pl.when((slot >= 0) & (keep[at] != 0))
        def _():
            change = jnp.dot(lower[slot], upper[at], preferred_element_type=jnp.float32)
            for half in range(2):
                rows = pl.ds(at * 2 + half, BLK, stride=8)
                out[rows, :] = out[rows, :] - change[:, half * 128 : half * 128 + 128]

        @pl.when((slot >= 0) & (hit[0] == at))
        def _():
            for half in range(2):
                out[pl.ds(at * 2 + half, BLK, stride=8), :] = lower[
                    slot, :, half * 128 : half * 128 + 128
                ].astype(jnp.float32)

        @pl.when((hit[1] == row) & (hit[0] == at))
        def _():
            for half in range(2):
                out[pl.ds(at * 2 + half, BLK, stride=8), :] = inverse[
                    :, half * 128 : half * 128 + 128
                ]


def finish(matrix, lower, upper, inverse, mask, slot_of, keep, hit):
    return pl.pallas_call(
        finish_kernel,
        grid_spec=pltpu.PrefetchScalarGridSpec(
            num_scalar_prefetch=4,
            grid=(8,),
            in_specs=[
                pl.BlockSpec((1, BLK, 4, BLK), lambda s, *_: (s, 0, 0, 0)),
                pl.BlockSpec((SLOTS, BLK, BLK), lambda s, *_: (0, 0, 0)),
                pl.BlockSpec((4, BLK, BLK), lambda s, *_: (0, 0, 0)),
                pl.BlockSpec((BLK, BLK), lambda s, *_: (0, 0)),
            ],
            out_specs=pl.BlockSpec((BLK * 8, 128), lambda s, *_: (s, 0)),
        ),
        out_shape=jax.ShapeDtypeStruct((8 * BLK * 8, 128), jnp.float32),
        name="finish",
        compiler_params=pltpu.CompilerParams(vmem_limit_bytes=32 * 1024 * 1024),
    )(mask, slot_of, keep, hit, matrix, lower, upper, inverse)


def places(size_row, size_col, core_zero, core_one):
    pairs = []
    for row in range(size_row):
        for at in range(size_col):
            to = (core_one if row % 2 else core_zero)(at // 8, at % 8)
            if to is not None:
                pairs.append((row * size_col + at, row * size_col + to[0] * 8 + to[1]))
    return pairs


def steps(parity):
    x1 = lambda x, z: (first(x), z)
    x2 = lambda x, z: (second(x, 4), z)
    mine = lambda z: z % 2 == parity
    z1 = lambda x, z: (x, first(z // 2) * 2 + parity) if mine(z) else None
    z2 = lambda x, z: (x, second(z // 2, 4) * 2 + parity) if mine(z) else None
    n1 = lambda x, z: (x, first(z))
    n2 = lambda x, z: (x, second(z, 8))
    across, along, last = (x1, x2), (z1, z2), (n1, n2)
    return [(across, along), (across, along), (along, across), (along, across), (last, last)]


def send_panel(parity, half_a, half_b, root_x, root_z):
    row, col = lax.axis_index("row"), lax.axis_index("col")
    sizes = lax.axis_size("row"), lax.axis_size("col")
    core, x, z = row % 2, col // 8, col % 8
    x_is = [x == root_x ^ 1, x == second_of(root_x, 4), x == root_x ^ 2]
    u, root_u = z // 2, root_z // 2
    z_is = [u == root_u ^ 1, u == second_of(root_u, 4), u == root_u ^ 2]
    early = [jnp.where(core == 0, a, b) for a, b in zip(x_is, z_is)]
    late = [jnp.where(core == 0, b, a) for a, b in zip(x_is, z_is)]
    plan = steps(parity)
    for step, (zero, one) in enumerate(plan):
        swap = step in (1, 3)
        got1 = lax.ppermute(half_b if swap else half_a, ("row", "col"), places(*sizes, zero[0], one[0]))
        got2 = lax.ppermute(half_a if swap else half_b, ("row", "col"), places(*sizes, zero[1], one[1]))
        near, far, opposite = early if step < 2 else late
        if step == 4:
            other = z % 2 != parity
            half_a, half_b = jnp.where(other, got1, half_a), jnp.where(other, got2, half_b)
        elif swap:
            half_b = jnp.where(near | opposite, got1, half_b)
            half_a = jnp.where(far | opposite, got2, half_a)
        else:
            half_a = jnp.where(near, got1, half_a)
            half_b = jnp.where(far, got2, half_b)
    return half_a, half_b


def row_pairs(size, to):
    return [(r, to(r // 2) * 2 + r % 2) for r in range(size)]


def body(matrix, pattern, panel):
    grid_row, grid_col = lax.axis_index("row"), lax.axis_index("col")
    rows_here, cols_here = lax.axis_size("row"), lax.axis_size("col")
    block_rows, order, block_cols = matrix.shape[0], matrix.shape[2], matrix.shape[3]
    at = panel[0]
    local = matrix.reshape(block_rows, order, block_cols, order)
    row_ids = jnp.arange(block_rows, dtype=jnp.int32) * rows_here + grid_row
    col_ids = jnp.arange(block_cols, dtype=jnp.int32) * cols_here + grid_col
    local_mask = lax.dynamic_index_in_dim(
        lax.dynamic_index_in_dim(
            pattern.reshape(block_rows, rows_here, block_cols, cols_here), grid_row, 1, keepdims=False
        ),
        grid_col,
        2,
        keepdims=False,
    )
    mask_top = lax.dynamic_index_in_dim(pattern, at, 0, keepdims=False).reshape(block_cols, cols_here)
    mask_top = lax.dynamic_index_in_dim(mask_top, grid_col, 1, keepdims=False)
    mask_left = lax.dynamic_index_in_dim(pattern, at, 1, keepdims=False).reshape(block_rows, rows_here)
    mask_left = lax.dynamic_index_in_dim(mask_left, grid_row, 1, keepdims=False)
    keep = ((mask_top != 0) & (col_ids > at)).astype(jnp.int32)
    used = (mask_left != 0) & (row_ids > at)
    count = jnp.cumsum(used.astype(jnp.int32))
    slot_of = jnp.where(used, count - 1, -1)
    numbers = jnp.arange(block_rows, dtype=jnp.int32)
    chosen = jnp.sum(
        jnp.where(slot_of[None, :] == jnp.arange(SLOTS, dtype=jnp.int32)[:, None], numbers[None, :], 0), axis=1
    )
    info = jnp.concatenate([jnp.stack([at // rows_here, at // cols_here]), chosen]).astype(jnp.int32)
    own_col = grid_col == at % cols_here
    hit = jnp.stack(
        [
            jnp.where(own_col, at // cols_here, -1),
            jnp.where(own_col & (grid_row == at % rows_here), at // rows_here, -1),
        ]
    ).astype(jnp.int32)
    col_hit = (jnp.arange(block_cols) == hit[0])[None, :] & (row_ids >= at)[:, None]
    mask = jnp.where(col_hit, 0, local_mask).reshape(-1).astype(jnp.int32)

    upper, pivot = extract_top(local, info)
    core, y = grid_row % 2, grid_row // 2
    root_core, root_y = at % rows_here % 2, at % rows_here // 2
    flip = [(r, r ^ 1) for r in range(rows_here)]
    y1 = row_pairs(rows_here, first)
    y2 = row_pairs(rows_here, lambda t: second(t, rows_here // 2))
    y3 = row_pairs(rows_here, lambda t: t ^ 2)
    y_is = [y == root_y ^ 1, y == second_of(root_y, 4), y == root_y ^ 2]

    pivot = jnp.where(core == root_core, pivot, lax.ppermute(pivot, "row", flip))
    pivot1, pivot2, pivot3 = (lax.ppermute(pivot, "row", p) for p in (y1, y2, y3))
    pivot = jnp.where(
        y_is[0], pivot1, jnp.where(y_is[1], pivot2, jnp.where(y_is[2], pivot3, pivot))
    )

    left = extract_left(local, info)
    inverse, lower = newton_lower(pivot, left)

    own = jnp.where(core == 0, upper[:2], upper[2:])
    other = jnp.where(core == 0, upper[2:], upper[:2])
    own = jnp.where(core == root_core, own, lax.ppermute(other, "row", flip))
    half_a, half_b = own[0], own[1]
    got1, got2 = lax.ppermute(half_a, "row", y1), lax.ppermute(half_b, "row", y2)
    half_a, half_b = jnp.where(y_is[0], got1, half_a), jnp.where(y_is[1], got2, half_b)
    got1, got2 = lax.ppermute(half_b, "row", y1), lax.ppermute(half_a, "row", y2)
    half_b = jnp.where(y_is[0] | y_is[2], got1, half_b)
    half_a = jnp.where(y_is[1] | y_is[2], got2, half_a)
    own = jnp.stack([half_a, half_b])
    other = lax.ppermute(own, "row", flip)
    upper = jnp.where(core == 0, jnp.concatenate([own, other]), jnp.concatenate([other, own]))

    flat = lower.reshape(2, SLOTS * order // 2, order)
    root_x, root_z = at % cols_here // 8, at % cols_here % 8
    half_a, half_b = lax.cond(
        root_z % 2 == 0,
        functools.partial(send_panel, 0),
        functools.partial(send_panel, 1),
        flat[0],
        flat[1],
        root_x,
        root_z,
    )
    lower = jnp.stack([half_a, half_b]).reshape(SLOTS, order, order)
    result = finish(local, lower, upper, inverse, mask, slot_of, keep, hit)
    return result.reshape(matrix.shape)


def solution(mesh):
    in_specs = (P(None, "row", None, None, "col", None), P(), P())
    out_specs = P(None, "row", None, None, "col", None)
    return jax.shard_map(body, mesh=mesh, in_specs=in_specs, out_specs=out_specs, check_vma=False)
```

time: 266 us -> 109 us (0.41)
  the two profiles are of different devices: /device:TPU:24 before, /device:TPU:1 now
where the time goes in v1:
time: 109 us; the launch traced here: 107 us
  starting transfers between devices  54.1 us (50%)
  Pallas kernels  18.5 us (17%)
  waiting for transfers between devices  18 us (17%)
  other arithmetic  8.37 us (8%)
  local copies, waits for them, and re-layouts  6.32 us (6%)
    ppermute x5, starting transfers between devices, send_panel(): lax.ppermute(half_b if swap else half_a, ('row', 'col'), places(*sizes, z...  22.3 us
    ppermute x5, starting transfers between devices, send_panel(): lax.ppermute(half_a if swap else half_b, ('row', 'col'), places(*sizes, z...  13.7 us
    ppermute x1, starting transfers between devices, body(): other = lax.ppermute(own, 'row', flip)  7.97 us
    ppermute x5, waiting for transfers between devices, send_panel(): lax.ppermute(half_a if swap else half_b, ('row', 'col'), places(*sizes, z...  7.82 us
    pallas_call x1, Pallas kernels, finish(): pl.pallas_call(finish_kernel, grid_spec=pltpu.PrefetchScalarGridSpec(num_...  6.53 us
    pallas_call x1, Pallas kernels, extract_left(): pl.pallas_call(left_kernel, grid_spec=pltpu.PrefetchScalarGridSpec(num_sc...  4.56 us
    pallas_call x1, Pallas kernels, newton_lower(): pl.pallas_call(newton_kernel, out_shape=[jax.ShapeDtypeStruct((BLK, BLK),...  4.41 us
    ppermute x1, waiting for transfers between devices, body(): lax.ppermute(half_b, 'row', y1)  4.17 us
  transfers between devices with their start and end apart: 20, of which 6 were waited for; matrix products, arithmetic and copies ran while one was open for 12% of the time, Pallas kernels for 8%

profile of v1, /device:TPU:1, one launch (start us, length us, event | category | flops | bytes accessed | tf_op | source)
XLA Modules:
  0.0 106.9 jit_solution(18362081330388771150)
XLA Ops:
  2.9 3.0 %extract_top.1 = (bf16[4,256,256]{2,1,0:T(8,128)(2,1)}, bf16[256,256]{1,0:T(8,128)(2,1)}) custom-call(s32[7]{0:T(128)} %pad_add_fusion.1.info, bf16[8,256,4,256]{3,2,1,0:T(4,128)(2,1)} %bitcast.41), custom_call_target="tpu_custom_call" | custom-call | tf_op jit(solution)/shard_map/extract_top/pallas_call | solution.py:49
  5.9 3.2 %collective-permute-start.20 = (bf16[256,256]{1,0:T(8,128)(2,1)}, bf16[256,256]{1,0:T(8,128)(2,1)S(1)}, u32[]{:S(2)}, u32[]{:S(2)}) collective-permute-start(bf16[256,256]{1,0:T(8,128)(2,1)} %get-tuple-element.46), channel_id=1, source_target_pairs={{0,32},{32,0},{64,96},{96,64},{128,160},{160,128},{192,224},{224,1... | collective-permute-start | bytes 393224 | tf_op jit(solution)/shard_map/ppermute | solution.py:286
  12.9 4.6 %extract_left.1.panel = bf16[5,256,256]{2,1,0:T(8,128)(2,1)} custom-call(s32[7]{0:T(128)} %pad_add_fusion.1.info, bf16[8,256,4,256]{3,2,1,0:T(4,128)(2,1)} %bitcast.42), custom_call_target="tpu_custom_call" | custom-call | tf_op jit(solution)/shard_map/extract_left/pallas_call | solution.py:76
  18.4 1.3 %collective-permute-start.23 = (bf16[256,256]{1,0:T(8,128)(2,1)S(1)}, bf16[256,256]{1,0:T(8,128)(2,1)S(1)}, u32[]{:S(2)}, u32[]{:S(2)}) collective-permute-start(bf16[256,256]{1,0:T(8,128)(2,1)S(1)} %broadcast_select_fusion.18), channel_id=1, source_target_pairs={{0,128},{32,160},{64,192},{96,224},{128,0},{160,32},{192,64},{224,... | collective-permute-start | bytes 393224 | tf_op jit(solution)/shard_map/ppermute | solution.py:287
  21.2 1.1 select_select_fusion
  23.1 1.9 %collective-permute-start.27 = (bf16[256,256]{1,0:T(8,128)(2,1)S(1)}, bf16[256,256]{1,0:T(8,128)(2,1)S(1)}, u32[]{:S(2)}, u32[]{:S(2)}) collective-permute-start(bf16[256,256]{1,0:T(8,128)(2,1)S(1)} %get-tuple-element.62), channel_id=1, source_target_pairs={{0,192},{32,224},{64,128},{96,160},{128,64},{160,96},{192,0},{224,... | collective-permute-start | bytes 393224 | tf_op jit(solution)/shard_map/ppermute | solution.py:299
  25.5 2.7 %collective-permute-done.22 = bf16[256,256]{1,0:T(8,128)(2,1)S(1)} collective-permute-done((bf16[256,256]{1,0:T(8,128)(2,1)S(1)}, bf16[256,256]{1,0:T(8,128)(2,1)S(1)}, u32[]{:S(2)}, u32[]{:S(2)}) %collective-permute-start.22) | collective-permute-done | bytes 131104 | tf_op jit(solution)/shard_map/ppermute | solution.py:287
  28.9 4.4 %newton_lower.1 = (f32[256,256]{1,0:T(8,128)}, bf16[5,256,256]{2,1,0:T(8,128)(2,1)}) custom-call(bf16[256,256]{1,0:T(8,128)(2,1)} %select_select_fusion.1.pivot, bf16[5,256,256]{2,1,0:T(8,128)(2,1)} %extract_left.1.panel), custom_call_target="tpu_custom_call" | custom-call | tf_op jit(solution)/shard_map/newton_lower/pallas_call | solution.py:119
  33.4 1.1 %collective-permute-start.26 = (bf16[256,256]{1,0:T(8,128)(2,1)S(1)}, bf16[256,256]{1,0:T(8,128)(2,1)S(1)}, u32[]{:S(2)}, u32[]{:S(2)}) collective-permute-start(bf16[256,256]{1,0:T(8,128)(2,1)S(1)} %get-tuple-element.59), channel_id=1, source_target_pairs={{0,192},{32,224},{64,128},{96,160},{128,64},{160,96},{192,0},{224,... | collective-permute-start | bytes 393224 | tf_op jit(solution)/shard_map/ppermute | solution.py:301
  34.5 1.1 %slice_bitcast_fusion = (bf16[640,256]{1,0:T(8,128)(2,1)S(1)}, bf16[640,256]{1,0:T(8,128)(2,1)S(1)}) fusion(bf16[2,640,256]{2,1,0:T(8,128)(2,1)} %bitcast.45), kind=kLoop, calls=%fused_computation.18 | loop fusion | bytes 1310720 | tf_op jit(solution)/shard_map/squeeze | solution.py:315
  35.6 51.0 %conditional.1 = (pred[640,256]{1,0:T(8,128)(4,1)S(1)}, pred[640,256]{1,0:T(8,128)(4,1)S(1)}, bf16[640,256]{1,0:T(8,128)(2,1)}, bf16[640,256]{1,0:T(8,128)(2,1)}...) conditional(s32[]{:T(128)} %convert_element_type.12, ...), branch_computations={%region_2.3_spmd, %region_3.4_spmd} | conditional | flops 1310863 | bytes 22611764 | solution.py:310
  38.9 3.1 %collective-permute-start.2 = (bf16[640,256]{1,0:T(8,128)(2,1)S(1)}, bf16[640,256]{1,0:T(8,128)(2,1)S(1)}, u32[]{:S(2)}, u32[]{:S(2)}) collective-permute-start(bf16[640,256]{1,0:T(8,128)(2,1)S(1)} %broadcast_select_fusion.5), channel_id=1, source_target_pairs={{1,3},{3,1},{5,7},{7,5},{9,11},{11,9},{13,15},{15,13},{17,19},{19,... | collective-permute-start | bytes 983048 | tf_op jit(solution)/shard_map/cond/branch_0_fun/ppermute | solution.py:219
  42.1 3.7 %collective-permute-start.7 = (bf16[640,256]{1,0:T(8,128)(2,1)S(1)}, bf16[640,256]{1,0:T(8,128)(2,1)S(1)}, u32[]{:S(2)}, u32[]{:S(2)}) collective-permute-start(bf16[640,256]{1,0:T(8,128)(2,1)S(1)} %broadcast_select_fusion.1), channel_id=1, source_target_pairs={{1,7},{3,5},{5,3},{7,1},{9,15},{11,13},{13,11},{15,9},{17,23},{19,... | collective-permute-start | bytes 983048 | tf_op jit(solution)/shard_map/cond/branch_0_fun/ppermute | solution.py:220
  45.9 2.8 %collective-permute-done.2 = bf16[640,256]{1,0:T(8,128)(2,1)S(1)} collective-permute-done((bf16[640,256]{1,0:T(8,128)(2,1)S(1)}, bf16[640,256]{1,0:T(8,128)(2,1)S(1)}, u32[]{:S(2)}, u32[]{:S(2)}) %collective-permute-start.2) | collective-permute-done | bytes 327712 | tf_op jit(solution)/shard_map/cond/branch_0_fun/ppermute | solution.py:219
  48.6 4.4 %collective-permute-start.3 = (bf16[640,256]{1,0:T(8,128)(2,1)S(1)}, bf16[640,256]{1,0:T(8,128)(2,1)S(1)}, u32[]{:S(2)}, u32[]{:S(2)}) collective-permute-start(bf16[640,256]{1,0:T(8,128)(2,1)S(1)} %broadcast_select_fusion.6), channel_id=1, source_target_pairs={{1,7},{3,5},{5,3},{7,1},{9,15},{11,13},{13,11},{15,9},{17,23},{19,... | collective-permute-start | bytes 983048 | tf_op jit(solution)/shard_map/cond/branch_0_fun/ppermute | solution.py:220
  53.1 1.9 %collective-permute-start.8 = (bf16[640,256]{1,0:T(8,128)(2,1)S(1)}, bf16[640,256]{1,0:T(8,128)(2,1)S(1)}, u32[]{:S(2)}, u32[]{:S(2)}) collective-permute-start(bf16[640,256]{1,0:T(8,128)(2,1)S(1)} %broadcast_select_fusion.2), channel_id=1, source_target_pairs={{1,3},{3,1},{5,7},{7,5},{9,11},{11,9},{13,15},{15,13},{17,19},{19,... | collective-permute-start | bytes 983048 | tf_op jit(solution)/shard_map/cond/branch_0_fun/ppermute | solution.py:219
  55.0 5.0 %collective-permute-done.3 = bf16[640,256]{1,0:T(8,128)(2,1)S(1)} collective-permute-done((bf16[640,256]{1,0:T(8,128)(2,1)S(1)}, bf16[640,256]{1,0:T(8,128)(2,1)S(1)}, u32[]{:S(2)}, u32[]{:S(2)}) %collective-permute-start.3) | collective-permute-done | bytes 327712 | tf_op jit(solution)/shard_map/cond/branch_0_fun/ppermute | solution.py:220
  60.8 15.8 %collective-permute-start.4 = (bf16[640,256]{1,0:T(8,128)(2,1)}, bf16[640,256]{1,0:T(8,128)(2,1)}, u32[]{:S(2)}, u32[]{:S(2)}) collective-permute-start(bf16[640,256]{1,0:T(8,128)(2,1)} %broadcast_select_fusion.7), channel_id=1, source_target_pairs={{0,1},{1,0},{2,3},{3,2},{4,5},{5,4},{6,7},{7,6},{8,9},{9,8},{10,11... | collective-permute-start | bytes 983048 | tf_op jit(solution)/shard_map/cond/branch_0_fun/ppermute | solution.py:219
  77.4 4.2 %collective-permute-start.9 = (bf16[640,256]{1,0:T(8,128)(2,1)}, bf16[640,256]{1,0:T(8,128)(2,1)}, u32[]{:S(2)}, u32[]{:S(2)}) collective-permute-start(bf16[640,256]{1,0:T(8,128)(2,1)} %broadcast_select_fusion.3), channel_id=1, source_target_pairs={{0,7},{1,2},{2,1},{3,4},{4,3},{5,6},{6,5},{7,0},{8,15},{9,10},{10,... | collective-permute-start | bytes 983048 | tf_op jit(solution)/shard_map/cond/branch_0_fun/ppermute | solution.py:220
  83.5 2.8 %collective-permute-done.9 = bf16[640,256]{1,0:T(8,128)(2,1)} collective-permute-done((bf16[640,256]{1,0:T(8,128)(2,1)}, bf16[640,256]{1,0:T(8,128)(2,1)}, u32[]{:S(2)}, u32[]{:S(2)}) %collective-permute-start.9) | collective-permute-done | bytes 327712 | tf_op jit(solution)/shard_map/cond/branch_0_fun/ppermute | solution.py:220
  86.8 4.2 %collective-permute-done.28 = bf16[256,256]{1,0:T(8,128)(2,1)S(1)} collective-permute-done((bf16[256,256]{1,0:T(8,128)(2,1)S(1)}, bf16[256,256]{1,0:T(8,128)(2,1)S(1)}, u32[]{:S(2)}, u32[]{:S(2)}) %collective-permute-start.28) | collective-permute-done | bytes 131104 | tf_op jit(solution)/shard_map/ppermute | solution.py:301
  91.0 8.0 %collective-permute-start.29 = (bf16[2,256,256]{2,1,0:T(8,128)(2,1)S(1)}, bf16[2,256,256]{2,1,0:T(8,128)(2,1)S(1)}, u32[]{:S(2)}, u32[]{:S(2)}) collective-permute-start(bf16[2,256,256]{2,1,0:T(8,128)(2,1)S(1)} %pad_maximum_fusion.1), channel_id=1, source_target_pairs={{0,32},{32,0},{64,96},{96,64},{128,160},{160,128},{192,224},{224,1... | collective-permute-start | bytes 786440 | tf_op jit(solution)/shard_map/ppermute | solution.py:305
  99.0 1.1 %select_bitcast_fusion.1 = (bf16[1,640,256]{2,1,0:T(8,128)(2,1)S(1)}, bf16[1,640,256]{2,1,0:T(8,128)(2,1)S(1)}) fusion(pred[640,256]{1,0:T(8,128)(4,1)S(1)} %get-tuple-element.48, bf16[640,256]{1,0:T(8,128)(2,1)} %get-tuple-element.49, bf16[640,256]{1,0:T(8,128)(2,1)S(1)} %get-tuple-element.50, bf16[640,256]{1,0:T(8,128)(2,1)} %get-tuple-element.51, ...), kind=kLoop, calls=%fused_computation.21 | loop fusion | flops 327680 | bytes 2129920 | tf_op jit(solution)/shard_map/stack | solution.py:319
  100.4 6.5 %finish.1 = f32[16384,128]{1,0:T(8,128)} custom-call(s32[32]{0:T(128)S(1)} %broadcast_select_fusion.20.mask, s32[8]{0:T(128)S(1)} %and_select_fusion.slot_of, s32[4]{0:T(128)S(1)} %and_convert_fusion.keep, s32[2]{0:T(128)S(1)} %pad_add_fusion.hit, bf16[8,256,4,256]{3,2,1,0:T(4,128)(2,1)S(1)} %bitcast.43, bf16[5,256,256]{2,1,0:T(8,128)(2,1)S(1)} %bitcast.44, ...), custom_call_target="tpu_custom_call" | custom-call | tf_op jit(solution)/shard_map/finish/pallas_call | solution.py:166
  (72 shorter events, 17.3 us)
Async XLA Ops:
  5.9 11.6 %collective-permute-start.20 = (bf16[256,256]{1,0:T(8,128)(2,1)}, bf16[256,256]{1,0:T(8,128)(2,1)S(1)}, u32[]{:S(2)}, u32[]{:S(2)}) collective-permute-start(bf16[256,256]{1,0:T(8,128)(2,1)} %get-tuple-element.46), channel_id=1, source_target_pairs={{0,32},{32,0},{64,96},{96,64},{128,160},{160,128},{192,224},{224,1... | collective-permute-start | bytes 393224 | tf_op jit(solution)/shard_map/ppermute | solution.py:286
  10.2 11.0 %collective-permute-start.24 = (bf16[2,256,256]{2,1,0:T(8,128)(2,1)S(1)}, bf16[2,256,256]{2,1,0:T(8,128)(2,1)S(1)}, u32[]{:S(2)}, u32[]{:S(2)}) collective-permute-start(bf16[2,256,256]{2,1,0:T(8,128)(2,1)S(1)} %broadcast_select_fusion.16), channel_id=1, source_target_pairs={{0,32},{32,0},{64,96},{96,64},{128,160},{160,128},{192,224},{224,1... | collective-permute-start | bytes 786440 | tf_op jit(solution)/shard_map/ppermute | solution.py:297
  18.4 7.1 %collective-permute-start.23 = (bf16[256,256]{1,0:T(8,128)(2,1)S(1)}, bf16[256,256]{1,0:T(8,128)(2,1)S(1)}, u32[]{:S(2)}, u32[]{:S(2)}) collective-permute-start(bf16[256,256]{1,0:T(8,128)(2,1)S(1)} %broadcast_select_fusion.18), channel_id=1, source_target_pairs={{0,128},{32,160},{64,192},{96,224},{128,0},{160,32},{192,64},{224,... | collective-permute-start | bytes 393224 | tf_op jit(solution)/shard_map/ppermute | solution.py:287
  19.7 8.6 %collective-permute-start.22 = (bf16[256,256]{1,0:T(8,128)(2,1)S(1)}, bf16[256,256]{1,0:T(8,128)(2,1)S(1)}, u32[]{:S(2)}, u32[]{:S(2)}) collective-permute-start(bf16[256,256]{1,0:T(8,128)(2,1)S(1)} %broadcast_select_fusion.18), channel_id=1, source_target_pairs={{0,192},{32,224},{64,128},{96,160},{128,64},{160,96},{192,0},{224,... | collective-permute-start | bytes 393224 | tf_op jit(solution)/shard_map/ppermute | solution.py:287
  20.5 7.8 %collective-permute-start.21 = (bf16[256,256]{1,0:T(8,128)(2,1)S(1)}, bf16[256,256]{1,0:T(8,128)(2,1)S(1)}, u32[]{:S(2)}, u32[]{:S(2)}) collective-permute-start(bf16[256,256]{1,0:T(8,128)(2,1)S(1)} %broadcast_select_fusion.18), channel_id=1, source_target_pairs={{0,64},{32,96},{64,0},{96,32},{128,192},{160,224},{192,128},{224,1... | collective-permute-start | bytes 393224 | tf_op jit(solution)/shard_map/ppermute | solution.py:287
  22.2 11.1 %collective-permute-start.25 = (bf16[256,256]{1,0:T(8,128)(2,1)S(1)}, bf16[256,256]{1,0:T(8,128)(2,1)S(1)}, u32[]{:S(2)}, u32[]{:S(2)}) collective-permute-start(bf16[256,256]{1,0:T(8,128)(2,1)S(1)} %get-tuple-element.61), channel_id=1, source_target_pairs={{0,64},{32,96},{64,0},{96,32},{128,192},{160,224},{192,128},{224,1... | collective-permute-start | bytes 393224 | tf_op jit(solution)/shard_map/ppermute | solution.py:299
  23.1 10.2 %collective-permute-start.27 = (bf16[256,256]{1,0:T(8,128)(2,1)S(1)}, bf16[256,256]{1,0:T(8,128)(2,1)S(1)}, u32[]{:S(2)}, u32[]{:S(2)}) collective-permute-start(bf16[256,256]{1,0:T(8,128)(2,1)S(1)} %get-tuple-element.62), channel_id=1, source_target_pairs={{0,192},{32,224},{64,128},{96,160},{128,64},{160,96},{192,0},{224,... | collective-permute-start | bytes 393224 | tf_op jit(solution)/shard_map/ppermute | solution.py:299
  33.4 53.4 %collective-permute-start.26 = (bf16[256,256]{1,0:T(8,128)(2,1)S(1)}, bf16[256,256]{1,0:T(8,128)(2,1)S(1)}, u32[]{:S(2)}, u32[]{:S(2)}) collective-permute-start(bf16[256,256]{1,0:T(8,128)(2,1)S(1)} %get-tuple-element.59), channel_id=1, source_target_pairs={{0,192},{32,224},{64,128},{96,160},{128,64},{160,96},{192,0},{224,... | collective-permute-start | bytes 393224 | tf_op jit(solution)/shard_map/ppermute | solution.py:301
  35.6 64.7 %copy-start.1 = (f32[256,256]{1,0:T(8,128)S(1)}, f32[256,256]{1,0:T(8,128)}, u32[]{:S(2)}) copy-start(f32[256,256]{1,0:T(8,128)} %get-tuple-element.54.inverse) | copy-start | bytes 786436
  35.7 1.7 %collective-permute-start = (bf16[640,256]{1,0:T(8,128)(2,1)S(1)}, bf16[640,256]{1,0:T(8,128)(2,1)S(1)}, u32[]{:S(2)}, u32[]{:S(2)}) collective-permute-start(bf16[640,256]{1,0:T(8,128)(2,1)S(1)} %get-tuple-element.31), channel_id=1, source_target_pairs={{0,8},{1,9},{2,10},{3,11},{4,12},{5,13},{6,14},{7,15},{8,0},{9,1},... | collective-permute-start | bytes 983048 | tf_op jit(solution)/shard_map/cond/branch_0_fun/ppermute | solution.py:219
  36.5 1.6 %collective-permute-start.5 = (bf16[640,256]{1,0:T(8,128)(2,1)S(1)}, bf16[640,256]{1,0:T(8,128)(2,1)S(1)}, u32[]{:S(2)}, u32[]{:S(2)}) collective-permute-start(bf16[640,256]{1,0:T(8,128)(2,1)S(1)} %get-tuple-element.32), channel_id=1, source_target_pairs={{0,24},{1,25},{2,26},{3,27},{4,28},{5,29},{6,30},{7,31},{8,16},{9,... | collective-permute-start | bytes 983048 | tf_op jit(solution)/shard_map/cond/branch_0_fun/ppermute | solution.py:220
  37.4 1.5 %collective-permute-start.1 = (bf16[640,256]{1,0:T(8,128)(2,1)S(1)}, bf16[640,256]{1,0:T(8,128)(2,1)S(1)}, u32[]{:S(2)}, u32[]{:S(2)}) collective-permute-start(bf16[640,256]{1,0:T(8,128)(2,1)S(1)} %broadcast_select_fusion.4), channel_id=1, source_target_pairs={{0,24},{1,25},{2,26},{3,27},{4,28},{5,29},{6,30},{7,31},{8,16},{9,... | collective-permute-start | bytes 983048 | tf_op jit(solution)/shard_map/cond/branch_0_fun/ppermute | solution.py:220
  38.1 3.9 %collective-permute-start.6 = (bf16[640,256]{1,0:T(8,128)(2,1)S(1)}, bf16[640,256]{1,0:T(8,128)(2,1)S(1)}, u32[]{:S(2)}, u32[]{:S(2)}) collective-permute-start(bf16[640,256]{1,0:T(8,128)(2,1)S(1)} %broadcast_select_fusion), channel_id=1, source_target_pairs={{0,8},{1,9},{2,10},{3,11},{4,12},{5,13},{6,14},{7,15},{8,0},{9,1},... | collective-permute-start | bytes 983048 | tf_op jit(solution)/shard_map/cond/branch_0_fun/ppermute | solution.py:219
  38.9 9.7 %collective-permute-start.2 = (bf16[640,256]{1,0:T(8,128)(2,1)S(1)}, bf16[640,256]{1,0:T(8,128)(2,1)S(1)}, u32[]{:S(2)}, u32[]{:S(2)}) collective-permute-start(bf16[640,256]{1,0:T(8,128)(2,1)S(1)} %broadcast_select_fusion.5), channel_id=1, source_target_pairs={{1,3},{3,1},{5,7},{7,5},{9,11},{11,9},{13,15},{15,13},{17,19},{19,... | collective-permute-start | bytes 983048 | tf_op jit(solution)/shard_map/cond/branch_0_fun/ppermute | solution.py:219
  42.1 10.9 %collective-permute-start.7 = (bf16[640,256]{1,0:T(8,128)(2,1)S(1)}, bf16[640,256]{1,0:T(8,128)(2,1)S(1)}, u32[]{:S(2)}, u32[]{:S(2)}) collective-permute-start(bf16[640,256]{1,0:T(8,128)(2,1)S(1)} %broadcast_select_fusion.1), channel_id=1, source_target_pairs={{1,7},{3,5},{5,3},{7,1},{9,15},{11,13},{13,11},{15,9},{17,23},{19,... | collective-permute-start | bytes 983048 | tf_op jit(solution)/shard_map/cond/branch_0_fun/ppermute | solution.py:220
  48.6 11.4 %collective-permute-start.3 = (bf16[640,256]{1,0:T(8,128)(2,1)S(1)}, bf16[640,256]{1,0:T(8,128)(2,1)S(1)}, u32[]{:S(2)}, u32[]{:S(2)}) collective-permute-start(bf16[640,256]{1,0:T(8,128)(2,1)S(1)} %broadcast_select_fusion.6), channel_id=1, source_target_pairs={{1,7},{3,5},{5,3},{7,1},{9,15},{11,13},{13,11},{15,9},{17,23},{19,... | collective-permute-start | bytes 983048 | tf_op jit(solution)/shard_map/cond/branch_0_fun/ppermute | solution.py:220
  53.1 23.5 %collective-permute-start.8 = (bf16[640,256]{1,0:T(8,128)(2,1)S(1)}, bf16[640,256]{1,0:T(8,128)(2,1)S(1)}, u32[]{:S(2)}, u32[]{:S(2)}) collective-permute-start(bf16[640,256]{1,0:T(8,128)(2,1)S(1)} %broadcast_select_fusion.2), channel_id=1, source_target_pairs={{1,3},{3,1},{5,7},{7,5},{9,11},{11,9},{13,15},{15,13},{17,19},{19,... | collective-permute-start | bytes 983048 | tf_op jit(solution)/shard_map/cond/branch_0_fun/ppermute | solution.py:219
  60.8 22.7 %collective-permute-start.4 = (bf16[640,256]{1,0:T(8,128)(2,1)}, bf16[640,256]{1,0:T(8,128)(2,1)}, u32[]{:S(2)}, u32[]{:S(2)}) collective-permute-start(bf16[640,256]{1,0:T(8,128)(2,1)} %broadcast_select_fusion.7), channel_id=1, source_target_pairs={{0,1},{1,0},{2,3},{3,2},{4,5},{5,4},{6,7},{7,6},{8,9},{9,8},{10,11... | collective-permute-start | bytes 983048 | tf_op jit(solution)/shard_map/cond/branch_0_fun/ppermute | solution.py:219
  77.4 9.0 %collective-permute-start.9 = (bf16[640,256]{1,0:T(8,128)(2,1)}, bf16[640,256]{1,0:T(8,128)(2,1)}, u32[]{:S(2)}, u32[]{:S(2)}) collective-permute-start(bf16[640,256]{1,0:T(8,128)(2,1)} %broadcast_select_fusion.3), channel_id=1, source_target_pairs={{0,7},{1,2},{2,1},{3,4},{4,3},{5,6},{6,5},{7,0},{8,15},{9,10},{10,... | collective-permute-start | bytes 983048 | tf_op jit(solution)/shard_map/cond/branch_0_fun/ppermute | solution.py:220
  86.6 13.7 %copy-start = (bf16[8,1,256,4,1,256]{5,3,4,2,1,0:T(4,128)(2,1)S(1)}, bf16[8,1,256,4,1,256]{5,3,4,2,1,0:T(4,128)(2,1)}, u32[]{:S(2)}) copy-start(bf16[8,1,256,4,1,256]{5,3,4,2,1,0:T(4,128)(2,1)} %param.5) | copy-start | bytes 12582916
  86.7 4.3 %collective-permute-start.28 = (bf16[256,256]{1,0:T(8,128)(2,1)S(1)}, bf16[256,256]{1,0:T(8,128)(2,1)S(1)}, u32[]{:S(2)}, u32[]{:S(2)}) collective-permute-start(bf16[256,256]{1,0:T(8,128)(2,1)S(1)} %get-tuple-element.60), channel_id=1, source_target_pairs={{0,64},{32,96},{64,0},{96,32},{128,192},{160,224},{192,128},{224,1... | collective-permute-start | bytes 393224 | tf_op jit(solution)/shard_map/ppermute | solution.py:301
  91.0 9.2 %collective-permute-start.29 = (bf16[2,256,256]{2,1,0:T(8,128)(2,1)S(1)}, bf16[2,256,256]{2,1,0:T(8,128)(2,1)S(1)}, u32[]{:S(2)}, u32[]{:S(2)}) collective-permute-start(bf16[2,256,256]{2,1,0:T(8,128)(2,1)S(1)} %pad_maximum_fusion.1), channel_id=1, source_target_pairs={{0,32},{32,0},{64,96},{96,64},{128,160},{160,128},{192,224},{224,1... | collective-permute-start | bytes 786440 | tf_op jit(solution)/shard_map/ppermute | solution.py:305

commit v2 on v1

v2 whole, which is shorter than its diff:
```python
import functools

import jax
import jax.numpy as jnp
from jax import lax
from jax.experimental import pallas as pl
from jax.experimental.pallas import tpu as pltpu
from jax.sharding import PartitionSpec as P

SLOTS = 5
BLK = 256
HALF = 128
WIDE_Z = 8


def first(t):
    return t ^ 1


def second(t, n):
    return (t + 1) % n if t % 2 else (t - 1) % n


def second_of(t, n):
    return jnp.where(t % 2 == 1, t + 1, t + n - 1) % n


def lanes(half):
    return slice(half * HALF, half * HALF + HALF)


def spread_rows(block, scratch):
    for half in range(2):
        scratch[:, half * 4 : half * 4 + 4, :] = block[:, :, lanes(half)].astype(jnp.float32)


def pivot_kernel(panel, place, block, mine, other, scratch):
    spread_rows(block[0], scratch)
    flat = scratch.reshape(BLK * 8, HALF)
    at = lax.div(panel[0], place[2])
    for half in range(2):
        for out, core in ((mine, place[0]), (other, 1 - place[0])):
            start = core * (HALF * 8) + half * 4 + at
            out[:, lanes(half)] = flat[pl.ds(start, HALF, stride=8), :].astype(jnp.bfloat16)


def extract_pivot(matrix, panel, place):
    half = jax.ShapeDtypeStruct((HALF, BLK), jnp.bfloat16)
    return pl.pallas_call(
        pivot_kernel,
        grid_spec=pltpu.PrefetchScalarGridSpec(
            num_scalar_prefetch=2,
            grid=(1,),
            in_specs=[pl.BlockSpec((1, BLK, 4, BLK), lambda s, panel, place: (lax.div(panel[0], place[1]), 0, 0, 0))],
            out_specs=[pl.BlockSpec((HALF, BLK), lambda s, *_: (0, 0))] * 2,
            scratch_shapes=[pltpu.VMEM((BLK, 8, HALF), jnp.float32)],
        ),
        out_shape=[half, half],
        name="extract_pivot",
    )(panel, place, matrix)


def upper_kernel(panel, place, block, mine_a, mine_b, other_a, other_b, scratch):
    spread_rows(block[0], scratch)
    flat = scratch.reshape(BLK * 8, HALF)
    core = place[0]
    for out, at in ((other_a, 2 - 2 * core), (other_b, 3 - 2 * core), (mine_a, 2 * core), (mine_b, 2 * core + 1)):
        for half in range(2):
            out[:, lanes(half)] = flat[pl.ds(half * 4 + at, BLK, stride=8), :].astype(jnp.bfloat16)


def extract_upper(matrix, panel, place):
    block = jax.ShapeDtypeStruct((BLK, BLK), jnp.bfloat16)
    return pl.pallas_call(
        upper_kernel,
        grid_spec=pltpu.PrefetchScalarGridSpec(
            num_scalar_prefetch=2,
            grid=(1,),
            in_specs=[pl.BlockSpec((1, BLK, 4, BLK), lambda s, panel, place: (lax.div(panel[0], place[1]), 0, 0, 0))],
            out_specs=[pl.BlockSpec((BLK, BLK), lambda s, *_: (0, 0))] * 4,
            scratch_shapes=[pltpu.VMEM((BLK, 8, HALF), jnp.float32)],
        ),
        out_shape=[block] * 4,
        name="extract_upper",
    )(panel, place, matrix)


def mask_kernel(mask, slot_at, used, hit, block, out, panel):
    row = pl.program_id(0)
    column = lax.broadcasted_iota(jnp.int32, (BLK, 4, HALF), 1)
    on = jnp.zeros((BLK, 4, HALF), jnp.int32)
    for at in range(4):
        on = jnp.where(column == at, mask[row * 4 + at], on)
    wide = out.reshape(BLK, 8, HALF)
    for half in range(2):
        piece = block[0, :, :, lanes(half)].astype(jnp.float32)
        wide[:, pl.ds(half, 4, stride=2), :] = jnp.where(on != 0, piece, 0.0)

    @pl.when(used[row] != 0)
    def _():
        for half in range(2):
            panel[0, :, lanes(half)] = out[pl.ds(hit[2] * 2 + half, BLK, stride=8), :].astype(jnp.bfloat16)

    @pl.when((hit[0] >= 0) & (row >= hit[3]))
    def _():
        for half in range(2):
            out[pl.ds(hit[2] * 2 + half, BLK, stride=8), :] = jnp.zeros((BLK, HALF), jnp.float32)


def mask_all(matrix, mask, slot_at, used, hit):
    return pl.pallas_call(
        mask_kernel,
        grid_spec=pltpu.PrefetchScalarGridSpec(
            num_scalar_prefetch=4,
            grid=(8,),
            in_specs=[pl.BlockSpec((1, BLK, 4, BLK), lambda s, *_: (s, 0, 0, 0))],
            out_specs=[
                pl.BlockSpec((BLK * 8, HALF), lambda s, *_: (s, 0)),
                pl.BlockSpec((1, BLK, BLK), lambda s, mask, slot_at, used, hit: (slot_at[s], 0, 0)),
            ],
        ),
        out_shape=[
            jax.ShapeDtypeStruct((8 * BLK * 8, HALF), jnp.float32),
            jax.ShapeDtypeStruct((SLOTS, BLK, BLK), jnp.bfloat16),
        ],
        name="mask_all",
        compiler_params=pltpu.CompilerParams(vmem_limit_bytes=24 * 1024 * 1024),
    )(mask, slot_at, used, hit, matrix)


def halves(value):
    high = value.astype(jnp.bfloat16)
    return high, (value - high.astype(jnp.float32)).astype(jnp.bfloat16)


def product(left, right):
    (left_high, left_low), (right_high, right_low) = left, right
    dot = functools.partial(jnp.dot, preferred_element_type=jnp.float32)
    return dot(left_high, right_high) + (dot(left_high, right_low) + dot(left_low, right_high))


def newton_kernel(place, mine, other, panel, inverse, lower_a, lower_b):
    own, rest = mine[...].astype(jnp.float32), other[...].astype(jnp.float32)
    zero = place[0] == 0
    block = jnp.concatenate([jnp.where(zero, own, rest), jnp.where(zero, rest, own)], axis=0)
    down = lax.broadcasted_iota(jnp.int32, (BLK, BLK), 0)
    along = lax.broadcasted_iota(jnp.int32, (BLK, BLK), 1)
    same = down == along
    identity = jnp.where(same, 1.0, 0.0)
    diagonal = jnp.where(same, block, 0.0)
    error = identity - block * (1.0 / jnp.sum(diagonal, axis=0, keepdims=True))
    error_parts = halves(error)
    error2 = product(error_parts, error_parts)
    error2_parts = halves(error2)
    error4 = product(error2_parts, error2_parts)
    left = identity + error
    left = left + error2 + product(error_parts, error2_parts)
    left = left + product(halves(left), halves(error4))
    result = left * (1.0 / jnp.sum(diagonal, axis=1, keepdims=True))
    inverse[...] = result
    high, low = halves(result)
    for slot in range(SLOTS):
        rows = panel[slot]
        total = jnp.dot(rows, low, preferred_element_type=jnp.float32)
        total += jnp.dot(rows, high, preferred_element_type=jnp.float32)
        lower_a[slot] = total[:HALF].astype(jnp.bfloat16)
        lower_b[slot] = total[HALF:].astype(jnp.bfloat16)


def newton_lower(place, mine, other, panel):
    half = jax.ShapeDtypeStruct((SLOTS, HALF, BLK), jnp.bfloat16)
    return pl.pallas_call(
        newton_kernel,
        in_specs=[pl.BlockSpec(memory_space=pltpu.SMEM)] + [pl.BlockSpec(memory_space=pltpu.VMEM)] * 3,
        out_shape=[jax.ShapeDtypeStruct((BLK, BLK), jnp.float32), half, half],
        name="newton_lower",
    )(place, mine, other, panel)


def update_kernel(rows, keep, hit, place, base, lower_a, lower_b, mine_a, mine_b, other_a, other_b, inverse, out):
    step = pl.program_id(0)
    row = rows[step]
    before = rows[jnp.maximum(step - 1, 0)]

    @pl.when((step == 0) | (row != before))
    def _():
        out[...] = base[...]

    live = (step > 0) & (step <= hit[4])
    slot = jnp.maximum(step - 1, 0)
    core = place[0]
    for at in range(4):
        own, others = ((mine_a, other_a), (mine_b, other_b))[at % 2]

        @pl.when(live & (keep[at] != 0))
        def _():
            right = jnp.where(core == at // 2, own[...], others[...])
            for part, lower in enumerate((lower_a, lower_b)):
                change = jnp.dot(lower[slot], right, preferred_element_type=jnp.float32)
                for half in range(2):
                    into = pl.ds(part * HALF * 8 + at * 2 + half, HALF, stride=8)
                    out[into, :] = out[into, :] - change[:, lanes(half)]

    @pl.when(live & (hit[0] >= 0))
    def _():
        for part, lower in enumerate((lower_a, lower_b)):
            for half in range(2):
                into = pl.ds(part * HALF * 8 + hit[2] * 2 + half, HALF, stride=8)
                out[into, :] = lower[slot, :, lanes(half)].astype(jnp.float32)

    @pl.when((step == 0) & (hit[1] != 0))
    def _():
        for half in range(2):
            out[pl.ds(hit[2] * 2 + half, BLK, stride=8), :] = inverse[:, lanes(half)]


def update(base, rows, keep, hit, place, lower, upper, inverse):
    whole = lambda *shape: pl.BlockSpec(shape, lambda s, *_: (0,) * len(shape))
    return pl.pallas_call(
        update_kernel,
        grid_spec=pltpu.PrefetchScalarGridSpec(
            num_scalar_prefetch=4,
            grid=(SLOTS + 1,),
            in_specs=[pl.BlockSpec((BLK * 8, HALF), lambda s, rows, *_: (rows[s], 0))]
            + [whole(SLOTS, HALF, BLK)] * 2
            + [whole(BLK, BLK)] * 5,
            out_specs=pl.BlockSpec((BLK * 8, HALF), lambda s, rows, *_: (rows[s], 0)),
        ),
        out_shape=jax.ShapeDtypeStruct(base.shape, jnp.float32),
        input_output_aliases={4: 0},
        name="update",
        compiler_params=pltpu.CompilerParams(vmem_limit_bytes=24 * 1024 * 1024),
    )(rows, keep, hit, place, base, *lower, *upper, inverse)


def places(size_row, size_col, core_zero, core_one):
    pairs = []
    for row in range(size_row):
        for at in range(size_col):
            to = (core_one if row % 2 else core_zero)(at // 8, at % 8)
            if to is not None:
                pairs.append((row * size_col + at, row * size_col + to[0] * 8 + to[1]))
    return pairs


def steps(parity):
    x1 = lambda x, z: (first(x), z)
    x2 = lambda x, z: (second(x, 4), z)
    mine = lambda z: z % 2 == parity
    z1 = lambda x, z: (x, first(z // 2) * 2 + parity) if mine(z) else None
    z2 = lambda x, z: (x, second(z // 2, 4) * 2 + parity) if mine(z) else None
    n1 = lambda x, z: (x, first(z))
    n2 = lambda x, z: (x, second(z, 8))
    across, along, last = (x1, x2), (z1, z2), (n1, n2)
    return [(across, along), (across, along), (along, across), (along, across), (last, last)]


def send_panel(parity, half_a, half_b, root_x, root_z):
    row, col = lax.axis_index("row"), lax.axis_index("col")
    sizes = lax.axis_size("row"), lax.axis_size("col")
    core, x, z = row % 2, col // 8, col % 8
    x_is = [x == root_x ^ 1, x == second_of(root_x, 4), x == root_x ^ 2]
    u, root_u = z // 2, root_z // 2
    z_is = [u == root_u ^ 1, u == second_of(root_u, 4), u == root_u ^ 2]
    early = [jnp.where(core == 0, a, b) for a, b in zip(x_is, z_is)]
    late = [jnp.where(core == 0, b, a) for a, b in zip(x_is, z_is)]
    plan = steps(parity)
    for step, (zero, one) in enumerate(plan):
        swap = step in (1, 3)
        got1 = lax.ppermute(half_b if swap else half_a, ("row", "col"), places(*sizes, zero[0], one[0]))
        got2 = lax.ppermute(half_a if swap else half_b, ("row", "col"), places(*sizes, zero[1], one[1]))
        near, far, opposite = early if step < 2 else late
        if step == 4:
            other = z % 2 != parity
            half_a, half_b = jnp.where(other, got1, half_a), jnp.where(other, got2, half_b)
        elif swap:
            half_b = jnp.where(near | opposite, got1, half_b)
            half_a = jnp.where(far | opposite, got2, half_a)
        else:
            half_a = jnp.where(near, got1, half_a)
            half_b = jnp.where(far, got2, half_b)
    return half_a, half_b


def body(matrix, pattern, panel):
    grid_row, grid_col = lax.axis_index("row"), lax.axis_index("col")
    rows_here, cols_here = lax.axis_size("row"), lax.axis_size("col")
    block_rows, order, block_cols = matrix.shape[0], matrix.shape[2], matrix.shape[3]
    at = panel[0]
    local = matrix.reshape(block_rows, order, block_cols, order)
    core, y = grid_row % 2, grid_row // 2
    root_core, root_y = at % rows_here % 2, at % rows_here // 2
    tall = rows_here // 2
    at_y = (y - root_y + tall) % tall
    place = jnp.stack([core, jnp.int32(rows_here), jnp.int32(cols_here)]).astype(jnp.int32)
    flip = [(r, r ^ 1) for r in range(rows_here)]
    shift = lambda value, by: lax.ppermute(
        value, "row", [(r, (r + 2 * by) % rows_here) for r in range(rows_here)]
    )
    cross = lambda value: lax.ppermute(value, "row", flip)

    pivot, pivot_other = extract_pivot(local, panel, place)
    pivot = jnp.where(core == root_core, pivot, cross(pivot_other))
    up, down, over = shift(pivot, 1), shift(pivot, -1), shift(pivot, 2)
    pivot = jnp.where(at_y == 1, up, jnp.where(at_y == 3, down, jnp.where(at_y == 2, over, pivot)))
    pivot_other = cross(pivot)

    row_ids = jnp.arange(block_rows, dtype=jnp.int32) * rows_here + grid_row
    col_ids = jnp.arange(block_cols, dtype=jnp.int32) * cols_here + grid_col
    local_mask = lax.dynamic_index_in_dim(
        lax.dynamic_index_in_dim(
            pattern.reshape(block_rows, rows_here, block_cols, cols_here), grid_row, 1, keepdims=False
        ),
        grid_col,
        2,
        keepdims=False,
    )
    mask = local_mask.reshape(-1).astype(jnp.int32)
    mask_top = lax.dynamic_index_in_dim(pattern, at, 0, keepdims=False).reshape(block_cols, cols_here)
    mask_top = lax.dynamic_index_in_dim(mask_top, grid_col, 1, keepdims=False)
    mask_left = lax.dynamic_index_in_dim(pattern, at, 1, keepdims=False).reshape(block_rows, rows_here)
    mask_left = lax.dynamic_index_in_dim(mask_left, grid_row, 1, keepdims=False)
    keep = ((mask_top != 0) & (col_ids > at)).astype(jnp.int32)
    used = ((mask_left != 0) & (row_ids > at)).astype(jnp.int32)
    numbers = jnp.arange(block_rows, dtype=jnp.int32)
    reached = jnp.sum(jnp.where(numbers[None, :] <= numbers[:, None], used[None, :], 0), axis=1)
    count = jnp.sum(used)
    slot_at = jnp.maximum(reached - 1, 0).astype(jnp.int32)
    owner_col = grid_col == at % cols_here
    owner = owner_col & (grid_row == at % rows_here)
    wanted = jnp.minimum(jnp.arange(SLOTS + 1, dtype=jnp.int32), count)
    wanted = jnp.where(wanted == 0, jnp.minimum(count, 1), wanted)
    rows = jnp.sum(
        jnp.where((reached[None, :] == wanted[:, None]) & (used[None, :] != 0), numbers[None, :], 0), axis=1
    )
    pivot_row = at // rows_here
    rows = jnp.where((jnp.arange(SLOTS + 1) == 0) | (count == 0), jnp.where(owner, pivot_row, rows), rows)
    rows = rows.astype(jnp.int32)
    first_below = (at - grid_row + rows_here - 1) // rows_here
    hit = jnp.stack(
        [jnp.where(owner_col, 1, -1), jnp.where(owner, 1, 0), at // cols_here, first_below, count]
    ).astype(jnp.int32)

    upper_a, upper_b, other_a, other_b = extract_upper(local, panel, place)
    from_a, from_b = cross(other_a), cross(other_b)
    upper_a = jnp.where(core == root_core, upper_a, from_a)
    upper_b = jnp.where(core == root_core, upper_b, from_b)
    up, down = shift(upper_a, 1), shift(upper_b, -1)
    upper_a, upper_b = jnp.where(at_y == 1, up, upper_a), jnp.where(at_y == 3, down, upper_b)
    is_root = at_y == 0
    up = shift(jnp.where(is_root, upper_b, upper_a), 1)
    down = shift(jnp.where(is_root, upper_a, upper_b), -1)
    upper_a = jnp.where(at_y == 2, up, jnp.where(at_y == 3, down, upper_a))
    upper_b = jnp.where(at_y == 1, up, jnp.where(at_y == 2, down, upper_b))
    other_a, other_b = cross(upper_a), cross(upper_b)

    base, left = mask_all(local, mask, slot_at, used, hit)
    inverse, lower_a, lower_b = newton_lower(place, pivot, pivot_other, left)

    root = at % cols_here
    root_x, root_z = root // WIDE_Z, root % WIDE_Z
    lower = lax.cond(
        root_z % 2 == 0,
        functools.partial(send_panel, 0),
        functools.partial(send_panel, 1),
        lower_a,
        lower_b,
        root_x,
        root_z,
    )
    result = update(base, rows, keep, hit, place, lower, (upper_a, upper_b, other_a, other_b), inverse)
    return result.reshape(matrix.shape)


def solution(mesh):
    in_specs = (P(None, "row", None, None, "col", None), P(), P())
    out_specs = P(None, "row", None, None, "col", None)
    return jax.shard_map(body, mesh=mesh, in_specs=in_specs, out_specs=out_specs, check_vma=False)
```

time: 109 us -> 108 us (level)
  the two profiles are of different devices: /device:TPU:1 before, /device:TPU:24 now
where the time goes in v2:
time: 108 us; the launch traced here: 107 us
  starting transfers between devices  48.2 us (45%)
  waiting for transfers between devices  26.3 us (24%)
  Pallas kernels  18.3 us (17%)
  other arithmetic  5.9 us (5%)
  local copies, waits for them, and re-layouts  5.28 us (5%)
  between operations  2.35 us (2%)
    ppermute x5, starting transfers between devices, send_panel(): lax.ppermute(half_a if swap else half_b, ('row', 'col'), places(*sizes, z...  22.1 us
    ppermute x5, starting transfers between devices, send_panel(): lax.ppermute(half_b if swap else half_a, ('row', 'col'), places(*sizes, z...  15.3 us
    ppermute x5, waiting for transfers between devices, send_panel(): lax.ppermute(half_b if swap else half_a, ('row', 'col'), places(*sizes, z...  10.9 us
    ppermute x7, starting transfers between devices, body(): lax.ppermute(value, 'row', [(r, (r + 2 * by) % rows_here) for r in range(...  9.61 us
    ppermute x5, waiting for transfers between devices, send_panel(): lax.ppermute(half_a if swap else half_b, ('row', 'col'), places(*sizes, z...  9.31 us
    ppermute x7, waiting for transfers between devices, body(): lax.ppermute(value, 'row', [(r, (r + 2 * by) % rows_here) for r in range(...  6.05 us
    pallas_call x1, Pallas kernels, mask_all(): pl.pallas_call(mask_kernel, grid_spec=pltpu.PrefetchScalarGridSpec(num_sc...  6 us
    pallas_call x1, Pallas kernels, update(): pl.pallas_call(update_kernel, grid_spec=pltpu.PrefetchScalarGridSpec(num_...  3.82 us
  transfers between devices with their start and end apart: 23, of which 9 were waited for; matrix products, arithmetic and copies ran while one was open for 6% of the time, Pallas kernels for 11%

profile of v2, /device:TPU:24, one launch (start us, length us, event | category | flops | bytes accessed | tf_op | source)
XLA Modules:
  0.0 106.8 jit_solution(15042907352148456009)
XLA Ops:
  1.3 2.7 %extract_pivot.1 = (bf16[128,256]{1,0:T(8,128)(2,1)}, bf16[128,256]{1,0:T(8,128)(2,1)}) custom-call(s32[1]{0:T(128)} %copy.17.panel, s32[3]{0:T(128)} %pad_add_fusion.place, bf16[8,256,4,256]{3,2,1,0:T(4,128)(2,1)} %bitcast.20), custom_call_target="tpu_custom_call" | custom-call | tf_op jit(solution)/shard_map/extract_pivot/pallas_call | solution.py:49
  3.9 2.9 %extract_upper.1 = (bf16[256,256]{1,0:T(8,128)(2,1)}, bf16[256,256]{1,0:T(8,128)(2,1)}, bf16[256,256]{1,0:T(8,128)(2,1)}, bf16[256,256]{1,0:T(8,128)(2,1)}) custom-call(s32[1]{0:T(128)} %copy.17.panel, s32[3]{0:T(128)} %pad_add_fusion.place, bf16[8,256,4,256]{3,2,1,0:T(4,128)(2,1)} %bitcast.21), custom_call_target="tpu_custom_call" | custom-call | tf_op jit(solution)/shard_map/extract_upper/pallas_call | solution.py:74
  14.0 2.6 %collective-permute-start.28 = (bf16[256,256]{1,0:T(8,128)(2,1)S(1)}, bf16[256,256]{1,0:T(8,128)(2,1)S(1)}, u32[]{:S(2)}, u32[]{:S(2)}) collective-permute-start(bf16[256,256]{1,0:T(8,128)(2,1)S(1)} %broadcast_select_fusion.21), channel_id=1, source_target_pairs={{0,64},{32,96},{64,128},{96,160},{128,192},{160,224},{192,0},{224,... | collective-permute-start | bytes 393224 | tf_op jit(solution)/shard_map/ppermute | solution.py:297
  19.1 1.8 %collective-permute-start.21 = (bf16[128,256]{1,0:T(8,128)(2,1)S(1)}, bf16[128,256]{1,0:T(8,128)(2,1)S(1)}, u32[]{:S(2)}, u32[]{:S(2)}) collective-permute-start(bf16[128,256]{1,0:T(8,128)(2,1)S(1)} %broadcast_select_fusion.26), channel_id=1, source_target_pairs={{0,64},{32,96},{64,128},{96,160},{128,192},{160,224},{192,0},{224,... | collective-permute-start | bytes 196616 | tf_op jit(solution)/shard_map/ppermute | solution.py:297
  21.1 2.7 %collective-permute-start.29 = (bf16[256,256]{1,0:T(8,128)(2,1)S(1)}, bf16[256,256]{1,0:T(8,128)(2,1)S(1)}, u32[]{:S(2)}, u32[]{:S(2)}) collective-permute-start(bf16[256,256]{1,0:T(8,128)(2,1)S(1)} %broadcast_select_fusion.25), channel_id=1, source_target_pairs={{0,64},{32,96},{64,128},{96,160},{128,192},{160,224},{192,0},{224,... | collective-permute-start | bytes 393224 | tf_op jit(solution)/shard_map/ppermute | solution.py:297
  24.1 2.2 %collective-permute-done.29 = bf16[256,256]{1,0:T(8,128)(2,1)S(1)} collective-permute-done((bf16[256,256]{1,0:T(8,128)(2,1)S(1)}, bf16[256,256]{1,0:T(8,128)(2,1)S(1)}, u32[]{:S(2)}, u32[]{:S(2)}) %collective-permute-start.29) | collective-permute-done | bytes 131104 | tf_op jit(solution)/shard_map/ppermute | solution.py:297
  26.3 3.7 %collective-permute-done.30 = bf16[256,256]{1,0:T(8,128)(2,1)S(1)} collective-permute-done((bf16[256,256]{1,0:T(8,128)(2,1)S(1)}, bf16[256,256]{1,0:T(8,128)(2,1)S(1)}, u32[]{:S(2)}, u32[]{:S(2)}) %collective-permute-start.30) | collective-permute-done | bytes 131104 | tf_op jit(solution)/shard_map/ppermute | solution.py:297
  31.9 2.2 %copy-done = bf16[8,1,256,4,1,256]{5,3,4,2,1,0:T(4,128)(2,1)S(1)} copy-done((bf16[8,1,256,4,1,256]{5,3,4,2,1,0:T(4,128)(2,1)S(1)}, bf16[8,1,256,4,1,256]{5,3,4,2,1,0:T(4,128)(2,1)}, u32[]{:S(2)}) %copy-start) | copy-done | bytes 4194328
  34.1 6.0 %mask_all.1 = (f32[16384,128]{1,0:T(8,128)}, bf16[5,256,256]{2,1,0:T(8,128)(2,1)S(1)}) custom-call(s32[32]{0:T(128)S(1)} %reshape.57.mask, s32[8]{0:T(128)S(1)} %add_maximum_fusion.slot_at, s32[8]{0:T(128)S(1)} %get-tuple-element.59.used, s32[5]{0:T(128)S(1)} %stack.29.hit, bf16[8,256,4,256]{3,2,1,0:T(4,128)(2,1)S(1)} %bitcast.22), custom_call_target="tpu_custom_call" | custom-call | tf_op jit(solution)/shard_map/mask_all/pallas_call | solution.py:111
  41.6 2.9 %newton_lower.1 = (f32[256,256]{1,0:T(8,128)}, bf16[5,128,256]{2,1,0:T(8,128)(2,1)S(1)}, bf16[5,128,256]{2,1,0:T(8,128)(2,1)S(1)}) custom-call(s32[3]{0:T(128)} %pad_add_fusion.place, bf16[128,256]{1,0:T(8,128)(2,1)} %copy-done.4, bf16[128,256]{1,0:T(8,128)(2,1)} %copy-done.6, bf16[5,256,256]{2,1,0:T(8,128)(2,1)} %copy-done.1), custom_call_target="tpu_custom_call" | custom-call | tf_op jit(solution)/shard_map/newton_lower/pallas_call | solution.py:172
  44.5 58.5 %conditional.1 = (bf16[5,128,256]{2,1,0:T(8,128)(2,1)S(1)}, bf16[5,128,256]{2,1,0:T(8,128)(2,1)S(1)}) conditional(s32[]{:T(128)} %convert_element_type.11, (s32[]{:T(128)}, s32[]{:T(128)}, bf16[5,128,256]{2,1,0:T(8,128)(2,1)S(1)}, bf16[5,128,256]{2,1,0:T(8,128)(2,1)S(1)}) %tuple.13, (s32[]{:T(128)}, s32[]{:T(128)}, ...), branch_computations={%region_3.4_spmd, %region_4.5_spmd} | conditional | flops 1638543 | bytes 22939392 | solution.py:362
  44.5 4.1 %collective-permute-start.10 = (bf16[5,128,256]{2,1,0:T(8,128)(2,1)S(1)}, bf16[5,128,256]{2,1,0:T(8,128)(2,1)S(1)}, u32[]{:S(2)}, u32[]{:S(2)}) collective-permute-start(bf16[5,128,256]{2,1,0:T(8,128)(2,1)S(1)} %get-tuple-element.27), channel_id=1, source_target_pairs={{0,8},{1,9},{2,10},{3,11},{4,12},{5,13},{6,14},{7,15},{8,0},{9,1},... | collective-permute-start | bytes 983048 | tf_op jit(solution)/shard_map/cond/branch_1_fun/ppermute | solution.py:270
  48.7 4.0 %collective-permute-start.15 = (bf16[5,128,256]{2,1,0:T(8,128)(2,1)S(1)}, bf16[5,128,256]{2,1,0:T(8,128)(2,1)S(1)}, u32[]{:S(2)}, u32[]{:S(2)}) collective-permute-start(bf16[5,128,256]{2,1,0:T(8,128)(2,1)S(1)} %get-tuple-element.28), channel_id=1, source_target_pairs={{0,24},{1,25},{2,26},{3,27},{4,28},{5,29},{6,30},{7,31},{8,16},{9,... | collective-permute-start | bytes 983048 | tf_op jit(solution)/shard_map/cond/branch_1_fun/ppermute | solution.py:271
  53.7 5.2 %collective-permute-start.11 = (bf16[5,128,256]{2,1,0:T(8,128)(2,1)S(1)}, bf16[5,128,256]{2,1,0:T(8,128)(2,1)S(1)}, u32[]{:S(2)}, u32[]{:S(2)}) collective-permute-start(bf16[5,128,256]{2,1,0:T(8,128)(2,1)S(1)} %broadcast_select_fusion.14), channel_id=1, source_target_pairs={{0,24},{1,25},{2,26},{3,27},{4,28},{5,29},{6,30},{7,31},{8,16},{9,... | collective-permute-start | bytes 983048 | tf_op jit(solution)/shard_map/cond/branch_1_fun/ppermute | solution.py:271
  59.0 2.1 %collective-permute-start.16 = (bf16[5,128,256]{2,1,0:T(8,128)(2,1)S(1)}, bf16[5,128,256]{2,1,0:T(8,128)(2,1)S(1)}, u32[]{:S(2)}, u32[]{:S(2)}) collective-permute-start(bf16[5,128,256]{2,1,0:T(8,128)(2,1)S(1)} %broadcast_select_fusion.10), channel_id=1, source_target_pairs={{0,8},{1,9},{2,10},{3,11},{4,12},{5,13},{6,14},{7,15},{8,0},{9,1},... | collective-permute-start | bytes 983048 | tf_op jit(solution)/shard_map/cond/branch_1_fun/ppermute | solution.py:270
  61.2 2.8 %collective-permute-done.11 = bf16[5,128,256]{2,1,0:T(8,128)(2,1)S(1)} collective-permute-done((bf16[5,128,256]{2,1,0:T(8,128)(2,1)S(1)}, bf16[5,128,256]{2,1,0:T(8,128)(2,1)S(1)}, u32[]{:S(2)}, u32[]{:S(2)}) %collective-permute-start.11) | collective-permute-done | bytes 327712 | tf_op jit(solution)/shard_map/cond/branch_1_fun/ppermute | solution.py:271
  64.0 5.6 %collective-permute-start.12 = (bf16[5,128,256]{2,1,0:T(8,128)(2,1)S(1)}, bf16[5,128,256]{2,1,0:T(8,128)(2,1)S(1)}, u32[]{:S(2)}, u32[]{:S(2)}) collective-permute-start(bf16[5,128,256]{2,1,0:T(8,128)(2,1)S(1)} %broadcast_select_fusion.15), channel_id=1, source_target_pairs={{0,2},{2,0},{4,6},{6,4},{8,10},{10,8},{12,14},{14,12},{16,18},{18,... | collective-permute-start | bytes 983048 | tf_op jit(solution)/shard_map/cond/branch_1_fun/ppermute | solution.py:270
  69.7 6.5 %collective-permute-start.17 = (bf16[5,128,256]{2,1,0:T(8,128)(2,1)S(1)}, bf16[5,128,256]{2,1,0:T(8,128)(2,1)S(1)}, u32[]{:S(2)}, u32[]{:S(2)}) collective-permute-start(bf16[5,128,256]{2,1,0:T(8,128)(2,1)S(1)} %broadcast_select_fusion.11), channel_id=1, source_target_pairs={{0,6},{2,4},{4,2},{6,0},{8,14},{10,12},{12,10},{14,8},{16,22},{18,... | collective-permute-start | bytes 983048 | tf_op jit(solution)/shard_map/cond/branch_1_fun/ppermute | solution.py:271
  76.3 6.3 %collective-permute-start.13 = (bf16[5,128,256]{2,1,0:T(8,128)(2,1)S(1)}, bf16[5,128,256]{2,1,0:T(8,128)(2,1)S(1)}, u32[]{:S(2)}, u32[]{:S(2)}) collective-permute-start(bf16[5,128,256]{2,1,0:T(8,128)(2,1)S(1)} %broadcast_select_fusion.16), channel_id=1, source_target_pairs={{0,6},{2,4},{4,2},{6,0},{8,14},{10,12},{12,10},{14,8},{16,22},{18,... | collective-permute-start | bytes 983048 | tf_op jit(solution)/shard_map/cond/branch_1_fun/ppermute | solution.py:271
  82.7 3.4 %collective-permute-start.18 = (bf16[5,128,256]{2,1,0:T(8,128)(2,1)S(1)}, bf16[5,128,256]{2,1,0:T(8,128)(2,1)S(1)}, u32[]{:S(2)}, u32[]{:S(2)}) collective-permute-start(bf16[5,128,256]{2,1,0:T(8,128)(2,1)S(1)} %broadcast_select_fusion.12), channel_id=1, source_target_pairs={{0,2},{2,0},{4,6},{6,4},{8,10},{10,8},{12,14},{14,12},{16,18},{18,... | collective-permute-start | bytes 983048 | tf_op jit(solution)/shard_map/cond/branch_1_fun/ppermute | solution.py:270
  87.8 6.7 %collective-permute-done.18 = bf16[5,128,256]{2,1,0:T(8,128)(2,1)S(1)} collective-permute-done((bf16[5,128,256]{2,1,0:T(8,128)(2,1)S(1)}, bf16[5,128,256]{2,1,0:T(8,128)(2,1)S(1)}, u32[]{:S(2)}, u32[]{:S(2)}) %collective-permute-start.18) | collective-permute-done | bytes 327712 | tf_op jit(solution)/shard_map/cond/branch_1_fun/ppermute | solution.py:270
  94.7 3.3 %collective-permute-done.14 = bf16[5,128,256]{2,1,0:T(8,128)(2,1)S(1)} collective-permute-done((bf16[5,128,256]{2,1,0:T(8,128)(2,1)S(1)}, bf16[5,128,256]{2,1,0:T(8,128)(2,1)S(1)}, u32[]{:S(2)}, u32[]{:S(2)}) %collective-permute-start.14) | collective-permute-done | bytes 327712 | tf_op jit(solution)/shard_map/cond/branch_1_fun/ppermute | solution.py:270
  98.0 4.9 %collective-permute-done.19 = bf16[5,128,256]{2,1,0:T(8,128)(2,1)S(1)} collective-permute-done((bf16[5,128,256]{2,1,0:T(8,128)(2,1)S(1)}, bf16[5,128,256]{2,1,0:T(8,128)(2,1)S(1)}, u32[]{:S(2)}, u32[]{:S(2)}) %collective-permute-start.19) | collective-permute-done | bytes 327712 | tf_op jit(solution)/shard_map/cond/branch_1_fun/ppermute | solution.py:271
  103.0 3.8 %update.1 = f32[16384,128]{1,0:T(8,128)} custom-call(s32[6]{0:T(128)S(1)} %or_select_fusion.rows, s32[4]{0:T(128)S(1)} %and_convert_fusion.keep, s32[5]{0:T(128)S(1)} %stack.29.hit, s32[3]{0:T(128)S(1)} %copy-done.3, f32[16384,128]{1,0:T(8,128)} %get-tuple-element.42.base, ...), custom_call_target="tpu_custom_call", output_to_operand_aliasing={{}: (4, {})} | custom-call | tf_op jit(solution)/shard_map/update/pallas_call | solution.py:219
  (78 shorter events, 15.5 us)
Async XLA Ops:
  3.9 12.7 %collective-permute-start.20 = (bf16[128,256]{1,0:T(8,128)(2,1)}, bf16[128,256]{1,0:T(8,128)(2,1)S(1)}, u32[]{:S(2)}, u32[]{:S(2)}) collective-permute-start(bf16[128,256]{1,0:T(8,128)(2,1)} %get-tuple-element.44), channel_id=1, source_target_pairs={{0,32},{32,0},{64,96},{96,64},{128,160},{160,128},{192,224},{224,1... | collective-permute-start | bytes 196616 | tf_op jit(solution)/shard_map/ppermute | solution.py:300
  6.9 4.5 %collective-permute-start.25 = (bf16[256,256]{1,0:T(8,128)(2,1)}, bf16[256,256]{1,0:T(8,128)(2,1)S(1)}, u32[]{:S(2)}, u32[]{:S(2)}) collective-permute-start(bf16[256,256]{1,0:T(8,128)(2,1)} %get-tuple-element.51), channel_id=1, source_target_pairs={{0,32},{32,0},{64,96},{96,64},{128,160},{160,128},{192,224},{224,1... | collective-permute-start | bytes 393224 | tf_op jit(solution)/shard_map/ppermute | solution.py:300
  7.4 5.7 %collective-permute-start.27 = (bf16[256,256]{1,0:T(8,128)(2,1)}, bf16[256,256]{1,0:T(8,128)(2,1)S(1)}, u32[]{:S(2)}, u32[]{:S(2)}) collective-permute-start(bf16[256,256]{1,0:T(8,128)(2,1)} %get-tuple-element.53), channel_id=1, source_target_pairs={{0,32},{32,0},{64,96},{96,64},{128,160},{160,128},{192,224},{224,1... | collective-permute-start | bytes 393224 | tf_op jit(solution)/shard_map/ppermute | solution.py:300
  12.3 8.7 %collective-permute-start.26 = (bf16[256,256]{1,0:T(8,128)(2,1)S(1)}, bf16[256,256]{1,0:T(8,128)(2,1)S(1)}, u32[]{:S(2)}, u32[]{:S(2)}) collective-permute-start(bf16[256,256]{1,0:T(8,128)(2,1)S(1)} %broadcast_select_fusion.22), channel_id=1, source_target_pairs={{0,192},{32,224},{64,0},{96,32},{128,64},{160,96},{192,128},{224,1... | collective-permute-start | bytes 393224 | tf_op jit(solution)/shard_map/ppermute | solution.py:297
  14.0 7.0 %collective-permute-start.28 = (bf16[256,256]{1,0:T(8,128)(2,1)S(1)}, bf16[256,256]{1,0:T(8,128)(2,1)S(1)}, u32[]{:S(2)}, u32[]{:S(2)}) collective-permute-start(bf16[256,256]{1,0:T(8,128)(2,1)S(1)} %broadcast_select_fusion.21), channel_id=1, source_target_pairs={{0,64},{32,96},{64,128},{96,160},{128,192},{160,224},{192,0},{224,... | collective-permute-start | bytes 393224 | tf_op jit(solution)/shard_map/ppermute | solution.py:297
  17.5 6.3 %collective-permute-start.23 = (bf16[128,256]{1,0:T(8,128)(2,1)S(1)}, bf16[128,256]{1,0:T(8,128)(2,1)S(1)}, u32[]{:S(2)}, u32[]{:S(2)}) collective-permute-start(bf16[128,256]{1,0:T(8,128)(2,1)S(1)} %broadcast_select_fusion.26), channel_id=1, source_target_pairs={{0,128},{32,160},{64,192},{96,224},{128,0},{160,32},{192,64},{224,... | collective-permute-start | bytes 196616 | tf_op jit(solution)/shard_map/ppermute | solution.py:297
  17.7 6.2 %collective-permute-start.22 = (bf16[128,256]{1,0:T(8,128)(2,1)S(1)}, bf16[128,256]{1,0:T(8,128)(2,1)S(1)}, u32[]{:S(2)}, u32[]{:S(2)}) collective-permute-start(bf16[128,256]{1,0:T(8,128)(2,1)S(1)} %broadcast_select_fusion.26), channel_id=1, source_target_pairs={{0,192},{32,224},{64,0},{96,32},{128,64},{160,96},{192,128},{224,1... | collective-permute-start | bytes 196616 | tf_op jit(solution)/shard_map/ppermute | solution.py:297
  19.1 4.8 %collective-permute-start.21 = (bf16[128,256]{1,0:T(8,128)(2,1)S(1)}, bf16[128,256]{1,0:T(8,128)(2,1)S(1)}, u32[]{:S(2)}, u32[]{:S(2)}) collective-permute-start(bf16[128,256]{1,0:T(8,128)(2,1)S(1)} %broadcast_select_fusion.26), channel_id=1, source_target_pairs={{0,64},{32,96},{64,128},{96,160},{128,192},{160,224},{192,0},{224,... | collective-permute-start | bytes 196616 | tf_op jit(solution)/shard_map/ppermute | solution.py:297
  21.1 5.2 %collective-permute-start.29 = (bf16[256,256]{1,0:T(8,128)(2,1)S(1)}, bf16[256,256]{1,0:T(8,128)(2,1)S(1)}, u32[]{:S(2)}, u32[]{:S(2)}) collective-permute-start(bf16[256,256]{1,0:T(8,128)(2,1)S(1)} %broadcast_select_fusion.25), channel_id=1, source_target_pairs={{0,64},{32,96},{64,128},{96,160},{128,192},{160,224},{192,0},{224,... | collective-permute-start | bytes 393224 | tf_op jit(solution)/shard_map/ppermute | solution.py:297
  23.8 6.2 %collective-permute-start.30 = (bf16[256,256]{1,0:T(8,128)(2,1)S(1)}, bf16[256,256]{1,0:T(8,128)(2,1)S(1)}, u32[]{:S(2)}, u32[]{:S(2)}) collective-permute-start(bf16[256,256]{1,0:T(8,128)(2,1)S(1)} %get-tuple-element.55), channel_id=1, source_target_pairs={{0,192},{32,224},{64,0},{96,32},{128,64},{160,96},{192,128},{224,1... | collective-permute-start | bytes 393224 | tf_op jit(solution)/shard_map/ppermute | solution.py:297
  24.0 17.0 %collective-permute-start.24 = (bf16[128,256]{1,0:T(8,128)(2,1)S(1)}, bf16[128,256]{1,0:T(8,128)(2,1)S(1)}, u32[]{:S(2)}, u32[]{:S(2)}) collective-permute-start(bf16[128,256]{1,0:T(8,128)(2,1)S(1)} %select_select_fusion.2.mine), channel_id=1, source_target_pairs={{0,32},{32,0},{64,96},{96,64},{128,160},{160,128},{192,224},{224,1... | collective-permute-start | bytes 196616 | tf_op jit(solution)/shard_map/ppermute | solution.py:300
  30.0 73.0 %collective-permute-start.32 = (bf16[256,256]{1,0:T(8,128)(2,1)S(1)}, bf16[256,256]{1,0:T(8,128)(2,1)S(1)}, u32[]{:S(2)}, u32[]{:S(2)}) collective-permute-start(bf16[256,256]{1,0:T(8,128)(2,1)S(1)} %get-tuple-element.60.mine_b), channel_id=1, source_target_pairs={{0,32},{32,0},{64,96},{96,64},{128,160},{160,128},{192,224},{224,1... | collective-permute-start | bytes 393224 | tf_op jit(solution)/shard_map/ppermute | solution.py:300
  30.1 72.9 %collective-permute-start.31 = (bf16[256,256]{1,0:T(8,128)(2,1)S(1)}, bf16[256,256]{1,0:T(8,128)(2,1)S(1)}, u32[]{:S(2)}, u32[]{:S(2)}) collective-permute-start(bf16[256,256]{1,0:T(8,128)(2,1)S(1)} %get-tuple-element.61.mine_a), channel_id=1, source_target_pairs={{0,32},{32,0},{64,96},{96,64},{128,160},{160,128},{192,224},{224,1... | collective-permute-start | bytes 393224 | tf_op jit(solution)/shard_map/ppermute | solution.py:300
  44.5 58.5 %copy-start.3 = (s32[3]{0:T(128)S(1)}, s32[3]{0:T(128)}, u32[]{:S(2)}) copy-start(s32[3]{0:T(128)} %pad_add_fusion.place) | copy-start | bytes 40
  44.5 9.2 %collective-permute-start.10 = (bf16[5,128,256]{2,1,0:T(8,128)(2,1)S(1)}, bf16[5,128,256]{2,1,0:T(8,128)(2,1)S(1)}, u32[]{:S(2)}, u32[]{:S(2)}) collective-permute-start(bf16[5,128,256]{2,1,0:T(8,128)(2,1)S(1)} %get-tuple-element.27), channel_id=1, source_target_pairs={{0,8},{1,9},{2,10},{3,11},{4,12},{5,13},{6,14},{7,15},{8,0},{9,1},... | collective-permute-start | bytes 983048 | tf_op jit(solution)/shard_map/cond/branch_1_fun/ppermute | solution.py:270
  48.7 10.3 %collective-permute-start.15 = (bf16[5,128,256]{2,1,0:T(8,128)(2,1)S(1)}, bf16[5,128,256]{2,1,0:T(8,128)(2,1)S(1)}, u32[]{:S(2)}, u32[]{:S(2)}) collective-permute-start(bf16[5,128,256]{2,1,0:T(8,128)(2,1)S(1)} %get-tuple-element.28), channel_id=1, source_target_pairs={{0,24},{1,25},{2,26},{3,27},{4,28},{5,29},{6,30},{7,31},{8,16},{9,... | collective-permute-start | bytes 983048 | tf_op jit(solution)/shard_map/cond/branch_1_fun/ppermute | solution.py:271
  53.7 10.2 %collective-permute-start.11 = (bf16[5,128,256]{2,1,0:T(8,128)(2,1)S(1)}, bf16[5,128,256]{2,1,0:T(8,128)(2,1)S(1)}, u32[]{:S(2)}, u32[]{:S(2)}) collective-permute-start(bf16[5,128,256]{2,1,0:T(8,128)(2,1)S(1)} %broadcast_select_fusion.14), channel_id=1, source_target_pairs={{0,24},{1,25},{2,26},{3,27},{4,28},{5,29},{6,30},{7,31},{8,16},{9,... | collective-permute-start | bytes 983048 | tf_op jit(solution)/shard_map/cond/branch_1_fun/ppermute | solution.py:271
  59.0 10.7 %collective-permute-start.16 = (bf16[5,128,256]{2,1,0:T(8,128)(2,1)S(1)}, bf16[5,128,256]{2,1,0:T(8,128)(2,1)S(1)}, u32[]{:S(2)}, u32[]{:S(2)}) collective-permute-start(bf16[5,128,256]{2,1,0:T(8,128)(2,1)S(1)} %broadcast_select_fusion.10), channel_id=1, source_target_pairs={{0,8},{1,9},{2,10},{3,11},{4,12},{5,13},{6,14},{7,15},{8,0},{9,1},... | collective-permute-start | bytes 983048 | tf_op jit(solution)/shard_map/cond/branch_1_fun/ppermute | solution.py:270
  64.0 12.2 %collective-permute-start.12 = (bf16[5,128,256]{2,1,0:T(8,128)(2,1)S(1)}, bf16[5,128,256]{2,1,0:T(8,128)(2,1)S(1)}, u32[]{:S(2)}, u32[]{:S(2)}) collective-permute-start(bf16[5,128,256]{2,1,0:T(8,128)(2,1)S(1)} %broadcast_select_fusion.15), channel_id=1, source_target_pairs={{0,2},{2,0},{4,6},{6,4},{8,10},{10,8},{12,14},{14,12},{16,18},{18,... | collective-permute-start | bytes 983048 | tf_op jit(solution)/shard_map/cond/branch_1_fun/ppermute | solution.py:270
  69.7 12.9 %collective-permute-start.17 = (bf16[5,128,256]{2,1,0:T(8,128)(2,1)S(1)}, bf16[5,128,256]{2,1,0:T(8,128)(2,1)S(1)}, u32[]{:S(2)}, u32[]{:S(2)}) collective-permute-start(bf16[5,128,256]{2,1,0:T(8,128)(2,1)S(1)} %broadcast_select_fusion.11), channel_id=1, source_target_pairs={{0,6},{2,4},{4,2},{6,0},{8,14},{10,12},{12,10},{14,8},{16,22},{18,... | collective-permute-start | bytes 983048 | tf_op jit(solution)/shard_map/cond/branch_1_fun/ppermute | solution.py:271
  76.3 11.4 %collective-permute-start.13 = (bf16[5,128,256]{2,1,0:T(8,128)(2,1)S(1)}, bf16[5,128,256]{2,1,0:T(8,128)(2,1)S(1)}, u32[]{:S(2)}, u32[]{:S(2)}) collective-permute-start(bf16[5,128,256]{2,1,0:T(8,128)(2,1)S(1)} %broadcast_select_fusion.16), channel_id=1, source_target_pairs={{0,6},{2,4},{4,2},{6,0},{8,14},{10,12},{12,10},{14,8},{16,22},{18,... | collective-permute-start | bytes 983048 | tf_op jit(solution)/shard_map/cond/branch_1_fun/ppermute | solution.py:271
  82.7 11.9 %collective-permute-start.18 = (bf16[5,128,256]{2,1,0:T(8,128)(2,1)S(1)}, bf16[5,128,256]{2,1,0:T(8,128)(2,1)S(1)}, u32[]{:S(2)}, u32[]{:S(2)}) collective-permute-start(bf16[5,128,256]{2,1,0:T(8,128)(2,1)S(1)} %broadcast_select_fusion.12), channel_id=1, source_target_pairs={{0,2},{2,0},{4,6},{6,4},{8,10},{10,8},{12,14},{14,12},{16,18},{18,... | collective-permute-start | bytes 983048 | tf_op jit(solution)/shard_map/cond/branch_1_fun/ppermute | solution.py:270
  87.7 10.3 %collective-permute-start.14 = (bf16[5,128,256]{2,1,0:T(8,128)(2,1)S(1)}, bf16[5,128,256]{2,1,0:T(8,128)(2,1)S(1)}, u32[]{:S(2)}, u32[]{:S(2)}) collective-permute-start(bf16[5,128,256]{2,1,0:T(8,128)(2,1)S(1)} %broadcast_select_fusion.17), channel_id=1, source_target_pairs={{0,1},{1,0},{2,3},{3,2},{4,5},{5,4},{6,7},{7,6},{8,9},{9,8},{10,11... | collective-permute-start | bytes 983048 | tf_op jit(solution)/shard_map/cond/branch_1_fun/ppermute | solution.py:270
  94.6 8.4 %collective-permute-start.19 = (bf16[5,128,256]{2,1,0:T(8,128)(2,1)S(1)}, bf16[5,128,256]{2,1,0:T(8,128)(2,1)S(1)}, u32[]{:S(2)}, u32[]{:S(2)}) collective-permute-start(bf16[5,128,256]{2,1,0:T(8,128)(2,1)S(1)} %broadcast_select_fusion.13), channel_id=1, source_target_pairs={{0,7},{1,2},{2,1},{3,4},{4,3},{5,6},{6,5},{7,0},{8,15},{9,10},{10,... | collective-permute-start | bytes 983048 | tf_op jit(solution)/shard_map/cond/branch_1_fun/ppermute | solution.py:271
  (6 other events, 86.5 us)

commit v3 on v2

--- a/solution.py
+++ b/solution.py
@@ -60,7 +60,7 @@
     )(panel, place, matrix)
 
 
-def upper_kernel(panel, place, block, mine_a, mine_b, other_a, other_b, scratch):
+def upper_kernel(panel, place, block, after, mine_a, mine_b, other_a, other_b, scratch):
     spread_rows(block[0], scratch)
     flat = scratch.reshape(BLK * 8, HALF)
     core = place[0]
@@ -69,20 +69,20 @@
             out[:, lanes(half)] = flat[pl.ds(half * 4 + at, BLK, stride=8), :].astype(jnp.bfloat16)
 
 
-def extract_upper(matrix, panel, place):
+def extract_upper(matrix, panel, place, after):
     block = jax.ShapeDtypeStruct((BLK, BLK), jnp.bfloat16)
     return pl.pallas_call(
         upper_kernel,
         grid_spec=pltpu.PrefetchScalarGridSpec(
             num_scalar_prefetch=2,
             grid=(1,),
-            in_specs=[pl.BlockSpec((1, BLK, 4, BLK), lambda s, panel, place: (lax.div(panel[0], place[1]), 0, 0, 0))],
+            in_specs=[pl.BlockSpec((1, BLK, 4, BLK), lambda s, panel, place: (lax.div(panel[0], place[1]), 0, 0, 0)), pl.BlockSpec(memory_space=pl.ANY)],
             out_specs=[pl.BlockSpec((BLK, BLK), lambda s, *_: (0, 0))] * 4,
             scratch_shapes=[pltpu.VMEM((BLK, 8, HALF), jnp.float32)],
         ),
         out_shape=[block] * 4,
         name="extract_upper",
-    )(panel, place, matrix)
+    )(panel, place, matrix, after)
 
 
 def mask_kernel(mask, slot_at, used, hit, block, out, panel):
@@ -124,6 +124,7 @@
             jax.ShapeDtypeStruct((SLOTS, BLK, BLK), jnp.bfloat16),
         ],
         name="mask_all",
+        cost_estimate=pl.CostEstimate(flops=4 << 20, bytes_accessed=20 << 20, transcendentals=0),
         compiler_params=pltpu.CompilerParams(vmem_limit_bytes=24 * 1024 * 1024),
     )(mask, slot_at, used, hit, matrix)
 
@@ -255,21 +256,41 @@
     return [(across, along), (across, along), (along, across), (along, across), (last, last)]
 
 
-def send_panel(parity, half_a, half_b, root_x, root_z):
+def row_moves(rows):
+    flip = [(r, r ^ 1) for r in range(rows)]
+    shift = lambda value, by: lax.ppermute(value, "row", [(r, (r + 2 * by) % rows) for r in range(rows)])
+    return lambda value: lax.ppermute(value, "row", flip), shift
+
+
+def send_all(parity, half_a, half_b, upper_a, upper_b, root_x, root_z, at_y):
     row, col = lax.axis_index("row"), lax.axis_index("col")
     sizes = lax.axis_size("row"), lax.axis_size("col")
-    core, x, z = row % 2, col // 8, col % 8
+    cross, shift = row_moves(sizes[0])
+    core, x, z = row % 2, col // WIDE_Z, col % WIDE_Z
     x_is = [x == root_x ^ 1, x == second_of(root_x, 4), x == root_x ^ 2]
     u, root_u = z // 2, root_z // 2
     z_is = [u == root_u ^ 1, u == second_of(root_u, 4), u == root_u ^ 2]
     early = [jnp.where(core == 0, a, b) for a, b in zip(x_is, z_is)]
     late = [jnp.where(core == 0, b, a) for a, b in zip(x_is, z_is)]
-    plan = steps(parity)
-    for step, (zero, one) in enumerate(plan):
+    is_root = at_y == 0
+    for step, (zero, one) in enumerate(steps(parity)):
         swap = step in (1, 3)
         got1 = lax.ppermute(half_b if swap else half_a, ("row", "col"), places(*sizes, zero[0], one[0]))
         got2 = lax.ppermute(half_a if swap else half_b, ("row", "col"), places(*sizes, zero[1], one[1]))
         near, far, opposite = early if step < 2 else late
+        if step == 0:
+            upper_a, got1 = lax.optimization_barrier((upper_a, got1))
+            up, down = shift(upper_a, 1), shift(upper_b, -1)
+            upper_a, upper_b = jnp.where(at_y == 1, up, upper_a), jnp.where(at_y == 3, down, upper_b)
+        if step == 1:
+            upper_a, got1 = lax.optimization_barrier((upper_a, got1))
+            up = shift(jnp.where(is_root, upper_b, upper_a), 1)
+            down = shift(jnp.where(is_root, upper_a, upper_b), -1)
+            upper_a = jnp.where(at_y == 2, up, jnp.where(at_y == 3, down, upper_a))
+            upper_b = jnp.where(at_y == 1, up, jnp.where(at_y == 2, down, upper_b))
+        if step == 3:
+            upper_a, got1 = lax.optimization_barrier((upper_a, got1))
+            other_a, other_b = cross(upper_a), cross(upper_b)
         if step == 4:
             other = z % 2 != parity
             half_a, half_b = jnp.where(other, got1, half_a), jnp.where(other, got2, half_b)
@@ -279,7 +300,7 @@
         else:
             half_a = jnp.where(near, got1, half_a)
             half_b = jnp.where(far, got2, half_b)
-    return half_a, half_b
+    return half_a, half_b, upper_a, upper_b, other_a, other_b
 
 
 def body(matrix, pattern, panel):
@@ -293,17 +314,10 @@
     tall = rows_here // 2
     at_y = (y - root_y + tall) % tall
     place = jnp.stack([core, jnp.int32(rows_here), jnp.int32(cols_here)]).astype(jnp.int32)
-    flip = [(r, r ^ 1) for r in range(rows_here)]
-    shift = lambda value, by: lax.ppermute(
-        value, "row", [(r, (r + 2 * by) % rows_here) for r in range(rows_here)]
-    )
-    cross = lambda value: lax.ppermute(value, "row", flip)
+    cross, shift = row_moves(rows_here)
 
     pivot, pivot_other = extract_pivot(local, panel, place)
     pivot = jnp.where(core == root_core, pivot, cross(pivot_other))
-    up, down, over = shift(pivot, 1), shift(pivot, -1), shift(pivot, 2)
-    pivot = jnp.where(at_y == 1, up, jnp.where(at_y == 3, down, jnp.where(at_y == 2, over, pivot)))
-    pivot_other = cross(pivot)
 
     row_ids = jnp.arange(block_rows, dtype=jnp.int32) * rows_here + grid_row
     col_ids = jnp.arange(block_cols, dtype=jnp.int32) * cols_here + grid_col
@@ -341,32 +355,29 @@
         [jnp.where(owner_col, 1, -1), jnp.where(owner, 1, 0), at // cols_here, first_below, count]
     ).astype(jnp.int32)
 
-    upper_a, upper_b, other_a, other_b = extract_upper(local, panel, place)
+    up, down, over = shift(pivot, 1), shift(pivot, -1), shift(pivot, 2)
+    upper_a, upper_b, other_a, other_b = extract_upper(local, panel, place, pivot)
+    base, left = mask_all(local, mask, slot_at, used, hit)
+    pivot = jnp.where(at_y == 1, up, jnp.where(at_y == 3, down, jnp.where(at_y == 2, over, pivot)))
+    pivot_other = cross(pivot)
     from_a, from_b = cross(other_a), cross(other_b)
+    inverse, lower_a, lower_b = newton_lower(place, pivot, pivot_other, left)
     upper_a = jnp.where(core == root_core, upper_a, from_a)
     upper_b = jnp.where(core == root_core, upper_b, from_b)
-    up, down = shift(upper_a, 1), shift(upper_b, -1)
-    upper_a, upper_b = jnp.where(at_y == 1, up, upper_a), jnp.where(at_y == 3, down, upper_b)
-    is_root = at_y == 0
-    up = shift(jnp.where(is_root, upper_b, upper_a), 1)
-    down = shift(jnp.where(is_root, upper_a, upper_b), -1)
-    upper_a = jnp.where(at_y == 2, up, jnp.where(at_y == 3, down, upper_a))
-    upper_b = jnp.where(at_y == 1, up, jnp.where(at_y == 2, down, upper_b))
-    other_a, other_b = cross(upper_a), cross(upper_b)
-
-    base, left = mask_all(local, mask, slot_at, used, hit)
-    inverse, lower_a, lower_b = newton_lower(place, pivot, pivot_other, left)
 
     root = at % cols_here
     root_x, root_z = root // WIDE_Z, root % WIDE_Z
-    lower = lax.cond(
+    *lower, upper_a, upper_b, other_a, other_b = lax.cond(
         root_z % 2 == 0,
-        functools.partial(send_panel, 0),
-        functools.partial(send_panel, 1),
+        functools.partial(send_all, 0),
+        functools.partial(send_all, 1),
         lower_a,
         lower_b,
+        upper_a,
+        upper_b,
         root_x,
         root_z,
+        at_y,
     )
     result = update(base, rows, keep, hit, place, lower, (upper_a, upper_b, other_a, other_b), inverse)
     return result.reshape(matrix.shape)

time: 108 us -> 103 us (0.954)
  starting transfers between devices: 48.2 us -> 42.5 us
  waiting for transfers between devices: 26.3 us -> 23 us
  local copies, waits for them, and re-layouts: 5.28 us -> 7.45 us
  Pallas kernels: 18.3 us -> 19.7 us
    ppermute x23, starting transfers between devices: 48.2 us -> 42.5 us  [the longest x5 18.5 us: send_all(): lax.ppermute(half_a if swap else half_b, ('row', 'col'), places(*sizes, z...]
    ppermute x23, waiting for transfers between devices: 26.3 us -> 23 us  [the longest x5 14.2 us: send_all(): lax.ppermute(half_a if swap else half_b, ('row', 'col'), places(*sizes, z...]
    pallas_call x1, Pallas kernels: 3.82 us -> 5.11 us  [update(): pl.pallas_call(update_kernel, grid_spec=pltpu.PrefetchScalarGridSpec(num_...]
  transfers between devices with their start and end apart: 23 -> 23, of which waited for: 9 -> 7; matrix products, arithmetic and copies ran while one was open for 6% -> 9% of each run, Pallas kernels for 11% -> 9%
where the time goes in v3:
time: 103 us; the launch traced here: 102 us
  starting transfers between devices  42.5 us (41%)
  waiting for transfers between devices  23 us (22%)
  Pallas kernels  19.7 us (19%)
  local copies, waits for them, and re-layouts  7.45 us (7%)
  other arithmetic  6.73 us (7%)
  between operations  2.3 us (2%)
    ppermute x5, starting transfers between devices, send_all(): lax.ppermute(half_a if swap else half_b, ('row', 'col'), places(*sizes, z...  18.5 us
    ppermute x5, starting transfers between devices, send_all(): lax.ppermute(half_b if swap else half_a, ('row', 'col'), places(*sizes, z...  14.3 us
    ppermute x5, waiting for transfers between devices, send_all(): lax.ppermute(half_a if swap else half_b, ('row', 'col'), places(*sizes, z...  14.2 us
    ppermute x7, starting transfers between devices, row_moves(): lax.ppermute(value, 'row', [(r, (r + 2 * by) % rows) for r in range(rows)])  8.51 us
    ppermute x5, waiting for transfers between devices, send_all(): lax.ppermute(half_b if swap else half_a, ('row', 'col'), places(*sizes, z...  7.86 us
    pallas_call x1, Pallas kernels, mask_all(): pl.pallas_call(mask_kernel, grid_spec=pltpu.PrefetchScalarGridSpec(num_sc...  6.06 us
    pallas_call x1, Pallas kernels, update(): pl.pallas_call(update_kernel, grid_spec=pltpu.PrefetchScalarGridSpec(num_...  5.11 us
    unnamed x14, local copies, waits for them, and re-layouts  3.64 us
  transfers between devices with their start and end apart: 23, of which 7 were waited for; matrix products, arithmetic and copies ran while one was open for 9% of the time, Pallas kernels for 9%

profile of v3, /device:TPU:24, one launch (start us, length us, event | category | flops | bytes accessed | tf_op | source)
XLA Modules:
  0.0 102.1 jit_solution(3465922608905866871)
XLA Ops:
  1.3 2.6 %extract_pivot.1 = (bf16[128,256]{1,0:T(8,128)(2,1)}, bf16[128,256]{1,0:T(8,128)(2,1)}) custom-call(s32[1]{0:T(128)} %copy.25.panel, s32[3]{0:T(128)} %pad_add_fusion.place, bf16[8,256,4,256]{3,2,1,0:T(4,128)(2,1)} %bitcast.20), custom_call_target="tpu_custom_call" | custom-call | tf_op jit(solution)/shard_map/extract_pivot/pallas_call | solution.py:49
  11.5 1.6 %collective-permute-start.34 = (bf16[128,256]{1,0:T(8,128)(2,1)S(1)}, bf16[128,256]{1,0:T(8,128)(2,1)S(1)}, u32[]{:S(2)}, u32[]{:S(2)}) collective-permute-start(bf16[128,256]{1,0:T(8,128)(2,1)S(1)} %broadcast_select_fusion.30.after), channel_id=1, source_target_pairs={{0,192},{32,224},{64,0},{96,32},{128,64},{160,96},{192,128},{224,1... | collective-permute-start | bytes 196616 | tf_op jit(solution)/shard_map/ppermute | solution.py:261
  13.1 1.7 %collective-permute-start.33 = (bf16[128,256]{1,0:T(8,128)(2,1)S(1)}, bf16[128,256]{1,0:T(8,128)(2,1)S(1)}, u32[]{:S(2)}, u32[]{:S(2)}) collective-permute-start(bf16[128,256]{1,0:T(8,128)(2,1)S(1)} %broadcast_select_fusion.30.after), channel_id=1, source_target_pairs={{0,64},{32,96},{64,128},{96,160},{128,192},{160,224},{192,0},{224,... | collective-permute-start | bytes 196616 | tf_op jit(solution)/shard_map/ppermute | solution.py:261
  16.9 2.2 %copy-done = bf16[8,1,256,4,1,256]{5,3,4,2,1,0:T(4,128)(2,1)S(1)} copy-done((bf16[8,1,256,4,1,256]{5,3,4,2,1,0:T(4,128)(2,1)S(1)}, bf16[8,1,256,4,1,256]{5,3,4,2,1,0:T(4,128)(2,1)}, u32[]{:S(2)}) %copy-start) | copy-done | bytes 4194328
  19.0 6.1 %mask_all.1 = (f32[16384,128]{1,0:T(8,128)}, bf16[5,256,256]{2,1,0:T(8,128)(2,1)S(1)}) custom-call(s32[32]{0:T(128)S(1)} %reshape.57.mask, s32[8]{0:T(128)S(1)} %add_maximum_fusion.slot_at, s32[8]{0:T(128)S(1)} %get-tuple-element.98.used, s32[5]{0:T(128)S(1)} %stack.29.hit, bf16[8,256,4,256]{3,2,1,0:T(4,128)(2,1)S(1)} %bitcast.22), custom_call_target="tpu_custom_call" | custom-call | flops 4194304 | bytes 20971520 | tf_op jit(solution)/shard_map/mask_all/pallas_call | solution.py:111
  25.9 2.9 %extract_upper.1 = (bf16[256,256]{1,0:T(8,128)(2,1)}, bf16[256,256]{1,0:T(8,128)(2,1)}, bf16[256,256]{1,0:T(8,128)(2,1)}, bf16[256,256]{1,0:T(8,128)(2,1)}) custom-call(s32[1]{0:T(128)} %copy.25.panel, s32[3]{0:T(128)} %pad_add_fusion.place, bf16[8,256,4,256]{3,2,1,0:T(4,128)(2,1)} %bitcast.21, bf16[128,256]{1,0:T(8,128)(2,1)} %copy-done.4), custom_call_target="tpu_custom_call" | custom-call | tf_op jit(solution)/shard_map/extract_upper/pallas_call | solution.py:74
  32.9 2.9 %newton_lower.1 = (f32[256,256]{1,0:T(8,128)}, bf16[5,128,256]{2,1,0:T(8,128)(2,1)S(1)}, bf16[5,128,256]{2,1,0:T(8,128)(2,1)S(1)}) custom-call(s32[3]{0:T(128)} %pad_add_fusion.place, bf16[128,256]{1,0:T(8,128)(2,1)} %copy-done.5, bf16[128,256]{1,0:T(8,128)(2,1)} %copy-done.6, bf16[5,256,256]{2,1,0:T(8,128)(2,1)} %copy-done.1), custom_call_target="tpu_custom_call" | custom-call | tf_op jit(solution)/shard_map/newton_lower/pallas_call | solution.py:173
  35.8 61.1 %conditional.1 = (bf16[5,128,256]{2,1,0:T(8,128)(2,1)S(1)}, bf16[5,128,256]{2,1,0:T(8,128)(2,1)S(1)}, bf16[256,256]{1,0:T(8,128)(2,1)}, bf16[256,256]{1,0:T(8,12...) conditional(s32[]{:T(128)} %convert_element_type.11, (s32[]{:T(128)}, s32[]{:T(128)}, ...), branch_computations={%region_3.4_spmd, %region_4.5_spmd} | conditional | flops 2162835 | bytes 28313656 | solution.py:370
  35.9 3.5 %collective-permute-start.16 = (bf16[5,128,256]{2,1,0:T(8,128)(2,1)S(1)}, bf16[5,128,256]{2,1,0:T(8,128)(2,1)S(1)}, u32[]{:S(2)}, u32[]{:S(2)}) collective-permute-start(bf16[5,128,256]{2,1,0:T(8,128)(2,1)S(1)} %get-tuple-element.49), channel_id=1, source_target_pairs={{0,8},{1,9},{2,10},{3,11},{4,12},{5,13},{6,14},{7,15},{8,0},{9,1},... | collective-permute-start | bytes 983048 | tf_op jit(solution)/shard_map/cond/branch_1_fun/ppermute | solution.py:278
  39.4 4.0 %collective-permute-start.23 = (bf16[5,128,256]{2,1,0:T(8,128)(2,1)S(1)}, bf16[5,128,256]{2,1,0:T(8,128)(2,1)S(1)}, u32[]{:S(2)}, u32[]{:S(2)}) collective-permute-start(bf16[5,128,256]{2,1,0:T(8,128)(2,1)S(1)} %get-tuple-element.54), channel_id=1, source_target_pairs={{0,24},{1,25},{2,26},{3,27},{4,28},{5,29},{6,30},{7,31},{8,16},{9,... | collective-permute-start | bytes 983048 | tf_op jit(solution)/shard_map/cond/branch_1_fun/ppermute | solution.py:279
  45.0 1.8 %collective-permute-start.22 = (bf16[256,256]{1,0:T(8,128)(2,1)S(1)}, bf16[256,256]{1,0:T(8,128)(2,1)S(1)}, u32[]{:S(2)}, u32[]{:S(2)}) collective-permute-start(bf16[256,256]{1,0:T(8,128)(2,1)S(1)} %get-tuple-element.53), channel_id=1, source_target_pairs={{0,64},{32,96},{64,128},{96,160},{128,192},{160,224},{192,0},{224,... | collective-permute-start | bytes 393224 | tf_op jit(solution)/shard_map/cond/branch_1_fun/ppermute | solution.py:261
  46.8 3.7 %collective-permute-start.17 = (bf16[5,128,256]{2,1,0:T(8,128)(2,1)S(1)}, bf16[5,128,256]{2,1,0:T(8,128)(2,1)S(1)}, u32[]{:S(2)}, u32[]{:S(2)}) collective-permute-start(bf16[5,128,256]{2,1,0:T(8,128)(2,1)S(1)} %broadcast_select_fusion.18), channel_id=1, source_target_pairs={{0,24},{1,25},{2,26},{3,27},{4,28},{5,29},{6,30},{7,31},{8,16},{9,... | collective-permute-start | bytes 983048 | tf_op jit(solution)/shard_map/cond/branch_1_fun/ppermute | solution.py:279
  50.6 2.1 %collective-permute-start.24 = (bf16[5,128,256]{2,1,0:T(8,128)(2,1)S(1)}, bf16[5,128,256]{2,1,0:T(8,128)(2,1)S(1)}, u32[]{:S(2)}, u32[]{:S(2)}) collective-permute-start(bf16[5,128,256]{2,1,0:T(8,128)(2,1)S(1)} %broadcast_select_fusion.16), channel_id=1, source_target_pairs={{0,8},{1,9},{2,10},{3,11},{4,12},{5,13},{6,14},{7,15},{8,0},{9,1},... | collective-permute-start | bytes 983048 | tf_op jit(solution)/shard_map/cond/branch_1_fun/ppermute | solution.py:278
  52.8 4.2 %collective-permute-done.17 = bf16[5,128,256]{2,1,0:T(8,128)(2,1)S(1)} collective-permute-done((bf16[5,128,256]{2,1,0:T(8,128)(2,1)S(1)}, bf16[5,128,256]{2,1,0:T(8,128)(2,1)S(1)}, u32[]{:S(2)}, u32[]{:S(2)}) %collective-permute-start.17) | collective-permute-done | bytes 327712 | tf_op jit(solution)/shard_map/cond/branch_1_fun/ppermute | solution.py:279
  57.0 5.2 %collective-permute-start.18 = (bf16[5,128,256]{2,1,0:T(8,128)(2,1)S(1)}, bf16[5,128,256]{2,1,0:T(8,128)(2,1)S(1)}, u32[]{:S(2)}, u32[]{:S(2)}) collective-permute-start(bf16[5,128,256]{2,1,0:T(8,128)(2,1)S(1)} %broadcast_select_fusion.19), channel_id=1, source_target_pairs={{0,2},{2,0},{4,6},{6,4},{8,10},{10,8},{12,14},{14,12},{16,18},{18,... | collective-permute-start | bytes 983048 | tf_op jit(solution)/shard_map/cond/branch_1_fun/ppermute | solution.py:278
  62.3 6.4 %collective-permute-start.27 = (bf16[5,128,256]{2,1,0:T(8,128)(2,1)S(1)}, bf16[5,128,256]{2,1,0:T(8,128)(2,1)S(1)}, u32[]{:S(2)}, u32[]{:S(2)}) collective-permute-start(bf16[5,128,256]{2,1,0:T(8,128)(2,1)S(1)} %broadcast_select_fusion.14), channel_id=1, source_target_pairs={{0,6},{2,4},{4,2},{6,0},{8,14},{10,12},{12,10},{14,8},{16,22},{18,... | collective-permute-start | bytes 983048 | tf_op jit(solution)/shard_map/cond/branch_1_fun/ppermute | solution.py:279
  69.0 1.8 %collective-permute-start.26 = (bf16[256,256]{1,0:T(8,128)(2,1)S(1)}, bf16[256,256]{1,0:T(8,128)(2,1)S(1)}, u32[]{:S(2)}, u32[]{:S(2)}) collective-permute-start(bf16[256,256]{1,0:T(8,128)(2,1)S(1)} %get-tuple-element.95), channel_id=1, source_target_pairs={{0,192},{32,224},{64,0},{96,32},{128,64},{160,96},{192,128},{224,1... | collective-permute-start | bytes 393224 | tf_op jit(solution)/shard_map/cond/branch_1_fun/ppermute | solution.py:261
  70.9 4.3 %collective-permute-start.19 = (bf16[5,128,256]{2,1,0:T(8,128)(2,1)S(1)}, bf16[5,128,256]{2,1,0:T(8,128)(2,1)S(1)}, u32[]{:S(2)}, u32[]{:S(2)}) collective-permute-start(bf16[5,128,256]{2,1,0:T(8,128)(2,1)S(1)} %broadcast_select_fusion.20), channel_id=1, source_target_pairs={{0,6},{2,4},{4,2},{6,0},{8,14},{10,12},{12,10},{14,8},{16,22},{18,... | collective-permute-start | bytes 983048 | tf_op jit(solution)/shard_map/cond/branch_1_fun/ppermute | solution.py:279
  75.2 3.4 %collective-permute-start.28 = (bf16[5,128,256]{2,1,0:T(8,128)(2,1)S(1)}, bf16[5,128,256]{2,1,0:T(8,128)(2,1)S(1)}, u32[]{:S(2)}, u32[]{:S(2)}) collective-permute-start(bf16[5,128,256]{2,1,0:T(8,128)(2,1)S(1)} %broadcast_select_fusion.15), channel_id=1, source_target_pairs={{0,2},{2,0},{4,6},{6,4},{8,10},{10,8},{12,14},{14,12},{16,18},{18,... | collective-permute-start | bytes 983048 | tf_op jit(solution)/shard_map/cond/branch_1_fun/ppermute | solution.py:278
  79.4 4.9 %collective-permute-done.19 = bf16[5,128,256]{2,1,0:T(8,128)(2,1)S(1)} collective-permute-done((bf16[5,128,256]{2,1,0:T(8,128)(2,1)S(1)}, bf16[5,128,256]{2,1,0:T(8,128)(2,1)S(1)}, u32[]{:S(2)}, u32[]{:S(2)}) %collective-permute-start.19) | collective-permute-done | bytes 327712 | tf_op jit(solution)/shard_map/cond/branch_1_fun/ppermute | solution.py:279
  84.4 4.1 %collective-permute-done.28 = bf16[5,128,256]{2,1,0:T(8,128)(2,1)S(1)} collective-permute-done((bf16[5,128,256]{2,1,0:T(8,128)(2,1)S(1)}, bf16[5,128,256]{2,1,0:T(8,128)(2,1)S(1)}, u32[]{:S(2)}, u32[]{:S(2)}) %collective-permute-start.28) | collective-permute-done | bytes 327712 | tf_op jit(solution)/shard_map/cond/branch_1_fun/ppermute | solution.py:278
  89.3 2.5 %collective-permute-done.20 = bf16[5,128,256]{2,1,0:T(8,128)(2,1)S(1)} collective-permute-done((bf16[5,128,256]{2,1,0:T(8,128)(2,1)S(1)}, bf16[5,128,256]{2,1,0:T(8,128)(2,1)S(1)}, u32[]{:S(2)}, u32[]{:S(2)}) %collective-permute-start.20) | collective-permute-done | bytes 327712 | tf_op jit(solution)/shard_map/cond/branch_1_fun/ppermute | solution.py:278
  91.8 5.1 %collective-permute-done.29 = bf16[5,128,256]{2,1,0:T(8,128)(2,1)S(1)} collective-permute-done((bf16[5,128,256]{2,1,0:T(8,128)(2,1)S(1)}, bf16[5,128,256]{2,1,0:T(8,128)(2,1)S(1)}, u32[]{:S(2)}, u32[]{:S(2)}) %collective-permute-start.29) | collective-permute-done | bytes 327712 | tf_op jit(solution)/shard_map/cond/branch_1_fun/ppermute | solution.py:279
  97.0 5.1 %update.1 = f32[16384,128]{1,0:T(8,128)} custom-call(s32[6]{0:T(128)S(1)} %or_select_fusion.rows, s32[4]{0:T(128)S(1)} %and_convert_fusion.keep, s32[5]{0:T(128)S(1)} %stack.29.hit, s32[3]{0:T(128)S(1)} %copy-done.3, f32[16384,128]{1,0:T(8,128)} %get-tuple-element.76.base, ...), custom_call_target="tpu_custom_call", output_to_operand_aliasing={{}: (4, {})} | custom-call | tf_op jit(solution)/shard_map/update/pallas_call | solution.py:220
  (79 shorter events, 17.3 us)
Async XLA Ops:
  4.0 5.4 %collective-permute-start.32 = (bf16[128,256]{1,0:T(8,128)(2,1)}, bf16[128,256]{1,0:T(8,128)(2,1)S(1)}, u32[]{:S(2)}, u32[]{:S(2)}) collective-permute-start(bf16[128,256]{1,0:T(8,128)(2,1)} %get-tuple-element.78), channel_id=1, source_target_pairs={{0,32},{32,0},{64,96},{96,64},{128,160},{160,128},{192,224},{224,1... | collective-permute-start | bytes 196616 | tf_op jit(solution)/shard_map/ppermute | solution.py:262
  10.2 19.2 %collective-permute-start.35 = (bf16[128,256]{1,0:T(8,128)(2,1)S(1)}, bf16[128,256]{1,0:T(8,128)(2,1)S(1)}, u32[]{:S(2)}, u32[]{:S(2)}) collective-permute-start(bf16[128,256]{1,0:T(8,128)(2,1)S(1)} %broadcast_select_fusion.30.after), channel_id=1, source_target_pairs={{0,128},{32,160},{64,192},{96,224},{128,0},{160,32},{192,64},{224,... | collective-permute-start | bytes 196616 | tf_op jit(solution)/shard_map/ppermute | solution.py:261
  11.5 17.9 %collective-permute-start.34 = (bf16[128,256]{1,0:T(8,128)(2,1)S(1)}, bf16[128,256]{1,0:T(8,128)(2,1)S(1)}, u32[]{:S(2)}, u32[]{:S(2)}) collective-permute-start(bf16[128,256]{1,0:T(8,128)(2,1)S(1)} %broadcast_select_fusion.30.after), channel_id=1, source_target_pairs={{0,192},{32,224},{64,0},{96,32},{128,64},{160,96},{192,128},{224,1... | collective-permute-start | bytes 196616 | tf_op jit(solution)/shard_map/ppermute | solution.py:261
  13.1 16.3 %collective-permute-start.33 = (bf16[128,256]{1,0:T(8,128)(2,1)S(1)}, bf16[128,256]{1,0:T(8,128)(2,1)S(1)}, u32[]{:S(2)}, u32[]{:S(2)}) collective-permute-start(bf16[128,256]{1,0:T(8,128)(2,1)S(1)} %broadcast_select_fusion.30.after), channel_id=1, source_target_pairs={{0,64},{32,96},{64,128},{96,160},{128,192},{160,224},{192,0},{224,... | collective-permute-start | bytes 196616 | tf_op jit(solution)/shard_map/ppermute | solution.py:261
  28.9 1.6 %collective-permute-start.37 = (bf16[256,256]{1,0:T(8,128)(2,1)}, bf16[256,256]{1,0:T(8,128)(2,1)S(1)}, u32[]{:S(2)}, u32[]{:S(2)}) collective-permute-start(bf16[256,256]{1,0:T(8,128)(2,1)} %get-tuple-element.82), channel_id=1, source_target_pairs={{0,32},{32,0},{64,96},{96,64},{128,160},{160,128},{192,224},{224,1... | collective-permute-start | bytes 393224 | tf_op jit(solution)/shard_map/ppermute | solution.py:262
  28.9 2.5 %collective-permute-start.38 = (bf16[256,256]{1,0:T(8,128)(2,1)}, bf16[256,256]{1,0:T(8,128)(2,1)S(1)}, u32[]{:S(2)}, u32[]{:S(2)}) collective-permute-start(bf16[256,256]{1,0:T(8,128)(2,1)} %get-tuple-element.84), channel_id=1, source_target_pairs={{0,32},{32,0},{64,96},{96,64},{128,160},{160,128},{192,224},{224,1... | collective-permute-start | bytes 393224 | tf_op jit(solution)/shard_map/ppermute | solution.py:262
  29.4 2.9 %collective-permute-start.36 = (bf16[128,256]{1,0:T(8,128)(2,1)S(1)}, bf16[128,256]{1,0:T(8,128)(2,1)S(1)}, u32[]{:S(2)}, u32[]{:S(2)}) collective-permute-start(bf16[128,256]{1,0:T(8,128)(2,1)S(1)} %select_select_fusion.4.mine), channel_id=1, source_target_pairs={{0,32},{32,0},{64,96},{96,64},{128,160},{160,128},{192,224},{224,1... | collective-permute-start | bytes 196616 | tf_op jit(solution)/shard_map/ppermute | solution.py:262
  35.8 61.1 %copy-start.3 = (s32[3]{0:T(128)S(1)}, s32[3]{0:T(128)}, u32[]{:S(2)}) copy-start(s32[3]{0:T(128)} %pad_add_fusion.place) | copy-start | bytes 40
  35.9 9.1 %collective-permute-start.16 = (bf16[5,128,256]{2,1,0:T(8,128)(2,1)S(1)}, bf16[5,128,256]{2,1,0:T(8,128)(2,1)S(1)}, u32[]{:S(2)}, u32[]{:S(2)}) collective-permute-start(bf16[5,128,256]{2,1,0:T(8,128)(2,1)S(1)} %get-tuple-element.49), channel_id=1, source_target_pairs={{0,8},{1,9},{2,10},{3,11},{4,12},{5,13},{6,14},{7,15},{8,0},{9,1},... | collective-permute-start | bytes 983048 | tf_op jit(solution)/shard_map/cond/branch_1_fun/ppermute | solution.py:278
  39.4 11.1 %collective-permute-start.23 = (bf16[5,128,256]{2,1,0:T(8,128)(2,1)S(1)}, bf16[5,128,256]{2,1,0:T(8,128)(2,1)S(1)}, u32[]{:S(2)}, u32[]{:S(2)}) collective-permute-start(bf16[5,128,256]{2,1,0:T(8,128)(2,1)S(1)} %get-tuple-element.54), channel_id=1, source_target_pairs={{0,24},{1,25},{2,26},{3,27},{4,28},{5,29},{6,30},{7,31},{8,16},{9,... | collective-permute-start | bytes 983048 | tf_op jit(solution)/shard_map/cond/branch_1_fun/ppermute | solution.py:279
  43.5 25.2 %collective-permute-start.21 = (bf16[256,256]{1,0:T(8,128)(2,1)S(1)}, bf16[256,256]{1,0:T(8,128)(2,1)S(1)}, u32[]{:S(2)}, u32[]{:S(2)}) collective-permute-start(bf16[256,256]{1,0:T(8,128)(2,1)S(1)} %get-tuple-element.52), channel_id=1, source_target_pairs={{0,192},{32,224},{64,0},{96,32},{128,64},{160,96},{192,128},{224,1... | collective-permute-start | bytes 393224 | tf_op jit(solution)/shard_map/cond/branch_1_fun/ppermute | solution.py:261
  45.0 7.8 %collective-permute-start.22 = (bf16[256,256]{1,0:T(8,128)(2,1)S(1)}, bf16[256,256]{1,0:T(8,128)(2,1)S(1)}, u32[]{:S(2)}, u32[]{:S(2)}) collective-permute-start(bf16[256,256]{1,0:T(8,128)(2,1)S(1)} %get-tuple-element.53), channel_id=1, source_target_pairs={{0,64},{32,96},{64,128},{96,160},{128,192},{160,224},{192,0},{224,... | collective-permute-start | bytes 393224 | tf_op jit(solution)/shard_map/cond/branch_1_fun/ppermute | solution.py:261
  46.8 10.2 %collective-permute-start.17 = (bf16[5,128,256]{2,1,0:T(8,128)(2,1)S(1)}, bf16[5,128,256]{2,1,0:T(8,128)(2,1)S(1)}, u32[]{:S(2)}, u32[]{:S(2)}) collective-permute-start(bf16[5,128,256]{2,1,0:T(8,128)(2,1)S(1)} %broadcast_select_fusion.18), channel_id=1, source_target_pairs={{0,24},{1,25},{2,26},{3,27},{4,28},{5,29},{6,30},{7,31},{8,16},{9,... | collective-permute-start | bytes 983048 | tf_op jit(solution)/shard_map/cond/branch_1_fun/ppermute | solution.py:279
  50.6 11.6 %collective-permute-start.24 = (bf16[5,128,256]{2,1,0:T(8,128)(2,1)S(1)}, bf16[5,128,256]{2,1,0:T(8,128)(2,1)S(1)}, u32[]{:S(2)}, u32[]{:S(2)}) collective-permute-start(bf16[5,128,256]{2,1,0:T(8,128)(2,1)S(1)} %broadcast_select_fusion.16), channel_id=1, source_target_pairs={{0,8},{1,9},{2,10},{3,11},{4,12},{5,13},{6,14},{7,15},{8,0},{9,1},... | collective-permute-start | bytes 983048 | tf_op jit(solution)/shard_map/cond/branch_1_fun/ppermute | solution.py:278
  57.0 13.8 %collective-permute-start.18 = (bf16[5,128,256]{2,1,0:T(8,128)(2,1)S(1)}, bf16[5,128,256]{2,1,0:T(8,128)(2,1)S(1)}, u32[]{:S(2)}, u32[]{:S(2)}) collective-permute-start(bf16[5,128,256]{2,1,0:T(8,128)(2,1)S(1)} %broadcast_select_fusion.19), channel_id=1, source_target_pairs={{0,2},{2,0},{4,6},{6,4},{8,10},{10,8},{12,14},{14,12},{16,18},{18,... | collective-permute-start | bytes 983048 | tf_op jit(solution)/shard_map/cond/branch_1_fun/ppermute | solution.py:278
  62.3 12.9 %collective-permute-start.27 = (bf16[5,128,256]{2,1,0:T(8,128)(2,1)S(1)}, bf16[5,128,256]{2,1,0:T(8,128)(2,1)S(1)}, u32[]{:S(2)}, u32[]{:S(2)}) collective-permute-start(bf16[5,128,256]{2,1,0:T(8,128)(2,1)S(1)} %broadcast_select_fusion.14), channel_id=1, source_target_pairs={{0,6},{2,4},{4,2},{6,0},{8,14},{10,12},{12,10},{14,8},{16,22},{18,... | collective-permute-start | bytes 983048 | tf_op jit(solution)/shard_map/cond/branch_1_fun/ppermute | solution.py:279
  68.8 9.9 %collective-permute-start.25 = (bf16[256,256]{1,0:T(8,128)(2,1)S(1)}, bf16[256,256]{1,0:T(8,128)(2,1)S(1)}, u32[]{:S(2)}, u32[]{:S(2)}) collective-permute-start(bf16[256,256]{1,0:T(8,128)(2,1)S(1)} %broadcast_select_fusion.27), channel_id=1, source_target_pairs={{0,64},{32,96},{64,128},{96,160},{128,192},{160,224},{192,0},{224,... | collective-permute-start | bytes 393224 | tf_op jit(solution)/shard_map/cond/branch_1_fun/ppermute | solution.py:261
  69.0 9.6 %collective-permute-start.26 = (bf16[256,256]{1,0:T(8,128)(2,1)S(1)}, bf16[256,256]{1,0:T(8,128)(2,1)S(1)}, u32[]{:S(2)}, u32[]{:S(2)}) collective-permute-start(bf16[256,256]{1,0:T(8,128)(2,1)S(1)} %get-tuple-element.95), channel_id=1, source_target_pairs={{0,192},{32,224},{64,0},{96,32},{128,64},{160,96},{192,128},{224,1... | collective-permute-start | bytes 393224 | tf_op jit(solution)/shard_map/cond/branch_1_fun/ppermute | solution.py:261
  70.9 13.3 %collective-permute-start.19 = (bf16[5,128,256]{2,1,0:T(8,128)(2,1)S(1)}, bf16[5,128,256]{2,1,0:T(8,128)(2,1)S(1)}, u32[]{:S(2)}, u32[]{:S(2)}) collective-permute-start(bf16[5,128,256]{2,1,0:T(8,128)(2,1)S(1)} %broadcast_select_fusion.20), channel_id=1, source_target_pairs={{0,6},{2,4},{4,2},{6,0},{8,14},{10,12},{12,10},{14,8},{16,22},{18,... | collective-permute-start | bytes 983048 | tf_op jit(solution)/shard_map/cond/branch_1_fun/ppermute | solution.py:279
  75.2 13.3 %collective-permute-start.28 = (bf16[5,128,256]{2,1,0:T(8,128)(2,1)S(1)}, bf16[5,128,256]{2,1,0:T(8,128)(2,1)S(1)}, u32[]{:S(2)}, u32[]{:S(2)}) collective-permute-start(bf16[5,128,256]{2,1,0:T(8,128)(2,1)S(1)} %broadcast_select_fusion.15), channel_id=1, source_target_pairs={{0,2},{2,0},{4,6},{6,4},{8,10},{10,8},{12,14},{14,12},{16,18},{18,... | collective-permute-start | bytes 983048 | tf_op jit(solution)/shard_map/cond/branch_1_fun/ppermute | solution.py:278
  84.3 7.4 %collective-permute-start.20 = (bf16[5,128,256]{2,1,0:T(8,128)(2,1)S(1)}, bf16[5,128,256]{2,1,0:T(8,128)(2,1)S(1)}, u32[]{:S(2)}, u32[]{:S(2)}) collective-permute-start(bf16[5,128,256]{2,1,0:T(8,128)(2,1)S(1)} %broadcast_select_fusion.21), channel_id=1, source_target_pairs={{0,1},{1,0},{2,3},{3,2},{4,5},{5,4},{6,7},{7,6},{8,9},{9,8},{10,11... | collective-permute-start | bytes 983048 | tf_op jit(solution)/shard_map/cond/branch_1_fun/ppermute | solution.py:278
  88.5 8.4 %collective-permute-start.29 = (bf16[5,128,256]{2,1,0:T(8,128)(2,1)S(1)}, bf16[5,128,256]{2,1,0:T(8,128)(2,1)S(1)}, u32[]{:S(2)}, u32[]{:S(2)}) collective-permute-start(bf16[5,128,256]{2,1,0:T(8,128)(2,1)S(1)} %broadcast_select_fusion.17), channel_id=1, source_target_pairs={{0,7},{1,2},{2,1},{3,4},{4,3},{5,6},{6,5},{7,0},{8,15},{9,10},{10,... | collective-permute-start | bytes 983048 | tf_op jit(solution)/shard_map/cond/branch_1_fun/ppermute | solution.py:279
  88.7 8.3 %collective-permute-start.31 = (bf16[256,256]{1,0:T(8,128)(2,1)}, bf16[256,256]{1,0:T(8,128)(2,1)}, u32[]{:S(2)}, u32[]{:S(2)}) collective-permute-start(bf16[256,256]{1,0:T(8,128)(2,1)} %get-tuple-element.112), channel_id=1, source_target_pairs={{0,32},{32,0},{64,96},{96,64},{128,160},{160,128},{192,224},{224,1... | collective-permute-start | bytes 393224 | tf_op jit(solution)/shard_map/cond/branch_1_fun/ppermute | solution.py:262
  88.8 8.2 %collective-permute-start.30 = (bf16[256,256]{1,0:T(8,128)(2,1)}, bf16[256,256]{1,0:T(8,128)(2,1)}, u32[]{:S(2)}, u32[]{:S(2)}) collective-permute-start(bf16[256,256]{1,0:T(8,128)(2,1)} %get-tuple-element.111), channel_id=1, source_target_pairs={{0,32},{32,0},{64,96},{96,64},{128,160},{160,128},{192,224},{224,1... | collective-permute-start | bytes 393224 | tf_op jit(solution)/shard_map/cond/branch_1_fun/ppermute | solution.py:262
  (6 other events, 82.6 us)
